TPU v7x, 256 devices: a whole 4x4x8 slice. The times are simulated.
256 devices in a mesh: leaf: 64 (over z_lo, y, x), rhs: 4 (over z_hi, core).
Axes of the slice: x: 4, y: 4, z: 8 (z_hi: 2, z_lo: 4; z = z_hi * 4 + z_lo), core: 2. Of those that a mesh axis runs over, the one named last changes fastest.
Arguments:
- charges: bfloat16 [1024, 8, 2, 256], P('leaf'), may hold values from -6 to 6
- near_blocks: bfloat16 [1024, 4, 2, 256, 256], P('leaf', 'rhs'), may hold values from -0.125 to 0.125
- near_list: int32 [1024, 4], P('leaf', 'rhs'), may hold values from 0 to 1023, as said below
- basis: bfloat16 [1024, 2, 128, 256], P('leaf'), may hold values from -0.25 to 0.25
- coupling: bfloat16 [1024, 4, 2, 128, 128], P('leaf'), may hold values from -0.1875 to 0.1875
- coupling_list: int32 [1024, 4], P('leaf'), may hold values from 0 to 1023, as said below
- transfer: bfloat16 [1024, 2, 128, 128], P('leaf'), may hold values from -0.1875 to 0.1875
- top_coupling: bfloat16 [256, 4, 2, 128, 128], P('leaf'), may hold values from -0.1875 to 0.1875
- top_list: int32 [256, 4], P('leaf'), may hold values from 0 to 255
Outputs:
- product: bfloat16 [1024, 8, 2, 256], P('leaf', 'rhs')
Inputs may be any that keep to these rules, and one draw needn't show every extreme that they name: `near_list`: every entry of row i lies within 16 leaves of i; entry 0 is i itself and entry 1 lies exactly 16 leaves from i. `coupling_list`: entry 0 of row i is (i + 512) modulo 1024; entry 1 lies exactly 16 leaves from i; every other entry lies 1 to 16 leaves from i.
All inputs are finite; a program needn't handle non-finite values.
Results may differ from a plain program's by a relative error of at most 0.0065.
Values may be sent and summed in bfloat16 or wider, within the bound.
No kernel may reach another device: no remote copies, remote signals or barrier semaphores. Data moves between devices by JAX's collectives and lax.ppermute only.
A program may use at most 64 MiB of HBM per device.

v0:
```python
import jax
import jax.numpy as jnp
from jax import lax
from jax.sharding import PartitionSpec as P


def with_halo(block, sides, width):
    for axis, dim in sides:
        count = lax.axis_size(axis)
        forward = [(i, i + 1) for i in range(count - 1)]
        backward = [(target, source) for source, target in forward]
        low = lax.ppermute(
            lax.slice_in_dim(block, block.shape[dim] - width, None, axis=dim), axis, forward
        )
        high = lax.ppermute(lax.slice_in_dim(block, 0, width, axis=dim), axis, backward)
        block = jnp.concatenate([low, block, high], axis=dim)
    return block


def combine(products):
    real_part = products[..., 0, 0, :] - products[..., 1, 1, :]
    imag_part = products[..., 0, 1, :] + products[..., 1, 0, :]
    return jnp.stack([real_part, imag_part], axis=-2)


def local(
    charges,
    near_blocks,
    near_list,
    basis,
    coupling,
    coupling_list,
    transfer,
    top_coupling,
    top_list,
):
    leaves = charges.shape[0]
    rhs_dev = charges.shape[1] // lax.axis_size("rhs")
    top_dev = top_coupling.shape[0]
    branch = leaves // top_dev
    rank = basis.shape[2]
    top_rank = transfer.shape[3]
    first_leaf = lax.axis_index("leaf") * leaves
    extended = with_halo(charges, (("leaf", 0),), leaves)
    own_rhs = lax.dynamic_slice_in_dim(charges, lax.axis_index("rhs") * rhs_dev, rhs_dev, 1)
    coefficients = combine(
        jnp.einsum("lakp,lrcp->lrack", basis, own_rhs, preferred_element_type=jnp.float32)
    ).astype(jnp.bfloat16)
    grouped = transfer.reshape(top_dev, branch, 2, rank, top_rank)
    children = coefficients.reshape(top_dev, branch, rhs_dev, 2, rank)
    parent_coef = combine(
        jnp.einsum("tbakq,tbrck->tracq", grouped, children, preferred_element_type=jnp.float32)
    ).astype(jnp.bfloat16)
    fetched = lax.all_gather(parent_coef, "leaf", axis=0, tiled=True)
    shard_rows = fetched.shape[0]
    selector = (
        top_list[:, :, None] == jnp.arange(shard_rows, dtype=jnp.int32)[None, None, :]
    ).astype(jnp.bfloat16)
    top_sources = jnp.einsum(
        "tmn,nrcq->tmrcq", selector, fetched, preferred_element_type=jnp.float32
    ).astype(jnp.bfloat16)
    top_field = combine(
        jnp.einsum(
            "tmaqs,tmrcs->tracq", top_coupling, top_sources, preferred_element_type=jnp.float32
        )
    ).astype(jnp.bfloat16)
    source_table = lax.all_gather(coefficients, "leaf", axis=0, tiled=True)
    sources = jnp.take(source_table, coupling_list, axis=0)
    leaf_field = combine(
        jnp.einsum("lmakj,lmrcj->lrack", coupling, sources, preferred_element_type=jnp.float32)
    )
    down_term = combine(
        jnp.einsum("tbakq,trcq->tbrack", grouped, top_field, preferred_element_type=jnp.float32)
    ).reshape(leaves, rhs_dev, 2, rank)
    field_coef = (leaf_field + down_term).astype(jnp.bfloat16)
    far_part = combine(
        jnp.einsum("lakp,lrck->lracp", basis, field_coef, preferred_element_type=jnp.float32)
    )
    near_sources = jnp.take(extended, near_list - first_leaf + leaves, axis=0)
    near_part = combine(
        jnp.einsum(
            "lmapq,lmrcq->lracp", near_blocks, near_sources, preferred_element_type=jnp.float32
        )
    )
    near_total = lax.psum_scatter(near_part, "rhs", scatter_dimension=1, tiled=True)
    return (far_part + near_total).astype(jnp.bfloat16)


def solution(mesh):
    return jax.shard_map(
        local,
        mesh=mesh,
        in_specs=(
            P("leaf", None, None, None),
            P("leaf", "rhs", None, None, None),
            P("leaf", "rhs"),
            P("leaf", None, None, None),
            P("leaf", None, None, None, None),
            P("leaf", None),
            P("leaf", None, None, None),
            P("leaf", None, None, None, None),
            P("leaf", None),
        ),
        out_specs=P("leaf", "rhs", None, None),
        check_vma=False,
    )
```

profile of v0, /device:TPU:2, one launch (start us, length us, event | category | flops | bytes accessed | tf_op | source)
XLA Modules:
  0.0 380.1 jit_solution(13142889988491532360)
XLA Ops:
  7.4 0.0 all-gather.2.cloned.1.call-start
  7.4 3.7 collective-permute-start
  11.1 2.4 collective-permute-start.1
  13.5 1.4 fusion.6
  15.0 0.6 copy.141
  15.6 0.0 all-gather.2.cloned.1.call-update
  15.7 0.0 reduce-scatter.2.cloned.1.call-start
  15.7 1.2 compare_and_fusion
  16.9 1.3 compare_select_fusion
  18.2 1.5 convolution_bitcast_fusion.2
  19.8 182.6 %all_gather.7 = bf16[256,2,2,128]{3,2,1,0:T(2,128)(2,1)S(1)} all-gather(bf16[4,2,2,128]{3,2,1,0:T(2,128)(2,1)S(1)} %copy.150), channel_id=1, replica_groups=mesh['leaf'=64,'rhs'=4] {'leaf'}, dimensions={0}, use_global_device_ids=true | all-gather | bytes 266240 | tf_op jit(solution)/shard_map/all_gather | solution.py:54
  202.4 0.9 fusion.17
  203.3 1.6 convolution_bitcast_fusion.1
  204.9 0.7 and_bitcast_fusion
  205.6 0.4 convolution_bitcast_fusion
  206.0 0.7 copy.139
  206.7 0.7 copy.142
  207.5 0.1 reshape.325
  207.6 0.5 pad_maximum_fusion
  208.2 0.8 gather_fusion.1
  209.0 0.2 fusion.26
  209.2 3.4 fusion.8
  212.7 0.8 copy.164
  213.5 0.0 reduce-scatter.2.cloned.1.call-update
  213.5 151.6 %all-gather.2.cloned.1.call-done = bf16[1024,2,2,128]{3,2,1,0:T(2,128)(2,1)} async-done(((bf16[16,2,2,128]{3,2,1,0:T(2,128)(2,1)}), bf16[1024,2,2,128]{3,2,1,0:T(2,128)(2,1)}) %all-gather.2.cloned.1.call-update) | async-done | bytes 1048592 | tf_op jit(solution)/shard_map/all_gather | solution.py:67
  365.1 1.9 gather_fusion
  367.1 3.4 fusion.14
  370.5 0.4 fusion.11
  370.9 0.1 fusion.31
  371.0 0.1 fusion.33
  371.1 0.0 reduce-scatter.2.cloned.1.call-done
  371.1 1.6 fusion.29
  (29 shorter events, 0.3 us)
Async XLA Ops:
  7.4 6.1 %copy-start = (bf16[16,2,128,256]{3,2,1,0:T(8,128)(2,1)S(1)}, bf16[16,2,128,256]{3,2,1,0:T(8,128)(2,1)}, u32[]{:S(2)}) copy-start(bf16[16,2,128,256]{3,2,1,0:T(8,128)(2,1)} %param.12) | copy-start | bytes 6291460
  7.4 200.3 %copy-start.2 = (bf16[16,8,2,256]{3,2,1,0:T(2,128)(2,1)S(1)}, bf16[16,8,2,256]{3,2,1,0:T(2,128)(2,1)}, u32[]{:S(2)}) copy-start(bf16[16,8,2,256]{3,2,1,0:T(2,128)(2,1)} %param.9) | copy-start | bytes 393220
  7.4 198.2 %copy-start.1 = (bf16[16,2,128,128]{3,2,1,0:T(8,128)(2,1)S(1)}, bf16[16,2,128,128]{3,2,1,0:T(8,128)(2,1)}, u32[]{:S(2)}) copy-start(bf16[16,2,128,128]{3,2,1,0:T(8,128)(2,1)} %param.15) | copy-start | bytes 3145732
  7.4 357.7 %all-gather.2.cloned.1.call-start = ((), (), s32[]{:S(2)}) async-start(), calls=%async_computation.1 | async-start | bytes 1064960 | tf_op jit(solution)/shard_map/all_gather | solution.py:67
  7.4 200.2 %collective-permute-start = (bf16[16,8,2,256]{3,2,1,0:T(2,128)(2,1)}, bf16[16,8,2,256]{3,2,1,0:T(2,128)(2,1)S(1)}, u32[]{:S(2)}, u32[]{:S(2)}) collective-permute-start(bf16[16,8,2,256]{3,2,1,0:T(2,128)(2,1)} %param.9), channel_id=1, source_target_pairs={{0,4},{4,8},{8,12},{12,16},{16,20},{20,24},{24,28},{28,32},{32,36}... | collective-permute-start | bytes 393224 | tf_op jit(solution)/shard_map/ppermute | solution.py:12
  11.1 196.6 %collective-permute-start.1 = (bf16[16,8,2,256]{3,2,1,0:T(2,128)(2,1)}, bf16[16,8,2,256]{3,2,1,0:T(2,128)(2,1)S(1)}, u32[]{:S(2)}, u32[]{:S(2)}) collective-permute-start(bf16[16,8,2,256]{3,2,1,0:T(2,128)(2,1)} %param.9), channel_id=1, source_target_pairs={{4,0},{8,4},{12,8},{16,12},{20,16},{24,20},{28,24},{32,28},{36,32}... | collective-permute-start | bytes 393224 | tf_op jit(solution)/shard_map/ppermute | solution.py:15
  15.7 355.4 %reduce-scatter.2.cloned.1.call-start = ((), (), s32[]{:S(2)}) async-start(), calls=%async_computation.2 | async-start | bytes 327680 | tf_op jit(solution)/shard_map/reduce_scatter | solution.py:85
Sparse Core Ops, SparseCore 0:
  15.8 349.2 all-gather.1
Sparse Core Ops, SparseCore 1:
  213.6 37.9 reduce-scatter.1
where the time goes:
time: 381 us; the launch traced here: 380 us
  blocking collectives  183 us (48%)
  waiting for transfers between devices  152 us (40%)
  between operations  15.1 us (4%)
  matrix products  13 us (3%)
  starting transfers between devices  6.16 us (2%)
  local copies, waits for them, and re-layouts  5.81 us (2%)
  other arithmetic  5.73 us (2%)
    all_gather x1, blocking collectives, local(): fetched = lax.all_gather(parent_coef, 'leaf', axis=0, tiled=True)  183 us
    all_gather x1, waiting for transfers between devices, local(): source_table = lax.all_gather(coefficients, 'leaf', axis=0, tiled=True)  152 us
  transfers between devices with their start and end apart: 4, of which 1 were waited for; matrix products, arithmetic and copies ran while one was open for 6% of the time, Pallas kernels for 0%

commit v1 on v0

v1 whole, which is shorter than its diff:
```python
import jax
import jax.numpy as jnp
from jax import lax
from jax.sharding import PartitionSpec as P


def shifted(value, axis, step):
    count = lax.axis_size(axis)
    return lax.ppermute(value, axis, [(i, (i - step) % count) for i in range(count)])


def flipped(value, axis, bit):
    count = lax.axis_size(axis)
    return lax.ppermute(value, axis, [(i, i ^ bit) for i in range(count)])


def combine(products):
    real_part = products[..., 0, 0, :] - products[..., 1, 1, :]
    imag_part = products[..., 0, 1, :] + products[..., 1, 0, :]
    return jnp.stack([real_part, imag_part], axis=-2)


def local(
    charges,
    near_blocks,
    near_list,
    basis,
    coupling,
    coupling_list,
    transfer,
    top_coupling,
    top_list,
):
    leaves, rhs_all, _, points = charges.shape
    rhs_dev = rhs_all // lax.axis_size("rhs")
    top_dev = top_coupling.shape[0]
    branch = leaves // top_dev
    rank = basis.shape[2]
    top_rank = transfer.shape[3]
    groups = lax.axis_size("leaf")
    me = lax.axis_index("leaf")
    rhs = lax.axis_index("rhs")
    first_leaf = me * leaves
    own_rhs = lax.dynamic_slice_in_dim(charges, rhs * rhs_dev, rhs_dev, 1)
    coefficients = combine(
        jnp.einsum("lakp,lrcp->lrack", basis, own_rhs, preferred_element_type=jnp.float32)
    ).astype(jnp.bfloat16)
    grouped = transfer.reshape(top_dev, branch, 2, rank, top_rank)
    children = coefficients.reshape(top_dev, branch, rhs_dev, 2, rank)
    parent_coef = combine(
        jnp.einsum("tbakq,tbrck->tracq", grouped, children, preferred_element_type=jnp.float32)
    ).astype(jnp.bfloat16)

    flat_parent = parent_coef.reshape(-1, rank)
    flat_coef = coefficients.reshape(-1, rank)
    parent_rows, coef_rows = flat_parent.shape[0], flat_coef.shape[0]
    packed = jnp.concatenate([flat_parent, flat_coef, charges.reshape(-1, rank)], axis=0)
    low = shifted(packed, "leaf", -1)
    high = shifted(packed, "leaf", 1)
    table = jnp.stack(
        [low[:parent_rows], flat_parent, high[:parent_rows], shifted(flat_parent, "leaf", 2)]
    )
    ends = parent_rows + coef_rows
    charge_halo = jnp.concatenate(
        [low[ends:].reshape(charges.shape), charges, high[ends:].reshape(charges.shape)]
    )

    near_sources = jnp.take(charge_halo, near_list - first_leaf + leaves, axis=0)
    near_part = combine(
        jnp.einsum(
            "lmapq,lmrcq->lracp", near_blocks, near_sources, preferred_element_type=jnp.float32
        )
    )

    flat_table = table.reshape(-1, rank)
    far_pack = shifted(jnp.concatenate([flat_table, flat_coef], axis=0), "leaf", groups // 2)
    table = jnp.stack(
        [
            shifted(flat_table, "leaf", -16),
            flat_table,
            shifted(flat_table, "leaf", 16),
            far_pack[: flat_table.shape[0]],
        ]
    )
    table = jnp.stack([shifted(table, "leaf", -4), table, shifted(table, "leaf", 4), shifted(table, "leaf", 8)])

    halves = near_part.reshape(leaves, 2, rhs_all // 2, 2, points)
    half = rhs // 2
    mine = lax.dynamic_index_in_dim(halves, half, 1, False)
    other = lax.dynamic_index_in_dim(halves, 1 - half, 1, False)
    mine = mine + flipped(other.astype(jnp.bfloat16), "rhs", 2).astype(jnp.float32)
    quarters = mine.reshape(leaves, 2, rhs_dev, 2, points)
    core = rhs % 2
    mine = lax.dynamic_index_in_dim(quarters, core, 1, False)
    other = lax.dynamic_index_in_dim(quarters, 1 - core, 1, False)
    near_total = mine + flipped(other.astype(jnp.bfloat16), "rhs", 1).astype(jnp.float32)

    coef_shape = coefficients.shape
    coef_table = jnp.concatenate(
        [
            low[parent_rows:ends].reshape(coef_shape),
            coefficients,
            high[parent_rows:ends].reshape(coef_shape),
            far_pack[flat_table.shape[0] :].reshape(coef_shape),
        ]
    )
    near_place = coupling_list - first_leaf + leaves
    far_place = coupling_list - (first_leaf + groups // 2 * leaves) % (groups * leaves) + 3 * leaves
    distant = jnp.arange(coupling_list.shape[1])[None, :] == 0
    place = jnp.where(distant, far_place, near_place)
    sources = jnp.take(coef_table, place, axis=0)
    leaf_field = combine(
        jnp.einsum("lmakj,lmrcj->lrack", coupling, sources, preferred_element_type=jnp.float32)
    )

    turn = (top_list // top_dev - me + 21) % groups
    row = (((turn // 4) % 4 * 4 + turn // 16) * 4 + turn % 4) * top_dev + top_list % top_dev
    top_sources = jnp.take(table.reshape(-1, rhs_dev, 2, top_rank), row, axis=0)
    top_field = combine(
        jnp.einsum(
            "tmaqs,tmrcs->tracq", top_coupling, top_sources, preferred_element_type=jnp.float32
        )
    ).astype(jnp.bfloat16)
    down_term = combine(
        jnp.einsum("tbakq,trcq->tbrack", grouped, top_field, preferred_element_type=jnp.float32)
    ).reshape(leaves, rhs_dev, 2, rank)
    field_coef = (leaf_field + down_term).astype(jnp.bfloat16)
    far_part = combine(
        jnp.einsum("lakp,lrck->lracp", basis, field_coef, preferred_element_type=jnp.float32)
    )
    return (far_part + near_total).astype(jnp.bfloat16)


def solution(mesh):
    return jax.shard_map(
        local,
        mesh=mesh,
        in_specs=(
            P("leaf", None, None, None),
            P("leaf", "rhs", None, None, None),
            P("leaf", "rhs"),
            P("leaf", None, None, None),
            P("leaf", None, None, None, None),
            P("leaf", None),
            P("leaf", None, None, None),
            P("leaf", None, None, None, None),
            P("leaf", None),
        ),
        out_specs=P("leaf", "rhs", None, None),
        check_vma=False,
    )
```

time: 381 us -> 62.2 us (0.16)
  the two profiles are of different devices: /device:TPU:2 before, /device:TPU:1 now
where the time goes in v1:
time: 62.2 us; the launch traced here: 60.9 us
  starting transfers between devices  22.9 us (37%)
  matrix products  12.1 us (19%)
  other arithmetic  10.4 us (17%)
  local copies, waits for them, and re-layouts  8.25 us (13%)
  waiting for transfers between devices  6.76 us (11%)
    ppermute x9, starting transfers between devices, shifted(): lax.ppermute(value, axis, [(i, (i - step) % count) for i in range(count)])  14.8 us
    ppermute x2, starting transfers between devices, flipped(): return lax.ppermute(value, axis, [(i, i ^ bit) for i in range(count)])  8.08 us
    ppermute x9, waiting for transfers between devices, shifted(): lax.ppermute(value, axis, [(i, (i - step) % count) for i in range(count)])  6.75 us
    dot_general x1, matrix products, local(): jnp.einsum('lmakj,lmrcj->lrack', coupling, sources, preferred_element_typ...  3.45 us
    dot_general x1, matrix products, local(): jnp.einsum('lmapq,lmrcq->lracp', near_blocks, near_sources, preferred_ele...  3.37 us
    unnamed x19, local copies, waits for them, and re-layouts  2.86 us
    another operation x2, other arithmetic, local(): jnp.stack([shifted(table, 'leaf', -4), table, shifted(table, 'leaf', 4),...  2.31 us
    dot_general x1, matrix products, local(): jnp.einsum('tmaqs,tmrcs->tracq', top_coupling, top_sources, preferred_ele...  1.61 us
  transfers between devices with their start and end apart: 11, of which 2 were waited for; matrix products, arithmetic and copies ran while one was open for 39% of the time, Pallas kernels for 0%

profile of v1, /device:TPU:1, one launch (start us, length us, event | category | flops | bytes accessed | tf_op | source)
XLA Modules:
  0.0 60.9 jit_solution(6343836669870871888)
XLA Ops:
  0.0 1.6 %copy-done = bf16[16,2,128,256]{3,2,1,0:T(8,128)(2,1)S(1)} copy-done((bf16[16,2,128,256]{3,2,1,0:T(8,128)(2,1)S(1)}, bf16[16,2,128,256]{3,2,1,0:T(8,128)(2,1)}, u32[]{:S(2)}) %copy-start) | copy-done | bytes 2097176
  1.6 1.4 %fusion.14 = f32[16,2,2,2,128]{4,3,2,1,0:T(2,128)S(1)} fusion(bf16[16,2,128,256]{3,2,1,0:T(8,128)(2,1)S(1)} %copy-done, bf16[16,8,2,256]{3,2,1,0:T(2,128)(2,1)} %param.9, s32[]{:T(128)S(6)} %select_n.97), kind=kOutput, calls=%fused_computation.13 | convolution fusion | flops 8388608 | bytes 2195460 | tf_op jit(solution)/shard_map/lakp,lrcp->lrack/dot_general | solution.py:46
  3.2 1.5 %convolution_bitcast_fusion.2 = f32[4,2,2,2,128]{4,3,2,1,0:T(2,128)S(1)} fusion(bf16[4,4,2,128,128,1]{4,3,2,1,0,5:T(8,128)(2,1)} %bitcast.170, bf16[4,4,2,1,128]{4,3,1,2,0:T(2,128)(2,1)S(1)} %copy.106, bf16[4,4,2,1,128]{4,3,1,2,0:T(2,128)(2,1)S(1)} %copy.105), kind=kOutput, calls=%fused_computation.17 | convolution fusion | flops 4227072 | bytes 1081344 | tf_op jit(solution)/shard_map/tbakq,tbrck->tracq/dot_general | solution.py:51
  4.8 10.2 %collective-permute-start.2 = (bf16[16,128]{1,0:T(8,128)(2,1)S(1)}, bf16[16,128]{1,0:T(8,128)(2,1)S(1)}, u32[]{:S(2)}, u32[]{:S(2)}) collective-permute-start(bf16[16,128]{1,0:T(8,128)(2,1)S(1)} %bitcast.194), channel_id=1, source_target_pairs={{0,248},{4,252},{8,0},{12,4},{16,8},{20,12},{24,16},{28,20},{32,24... | collective-permute-start | bytes 12296 | tf_op jit(solution)/shard_map/ppermute | solution.py:9
  14.9 1.0 %reshape.380 = bf16[512,128]{1,0:T(8,128)(2,1)S(1)} reshape(bf16[16,8,2,256]{3,2,1,0:T(2,128)(2,1)} %param.9) | data formatting | bytes 262144 | tf_op jit(solution)/shard_map/reshape | solution.py:57
  16.0 0.9 %collective-permute-start.1 = (bf16[592,128]{1,0:T(8,128)(2,1)S(1)}, bf16[592,128]{1,0:T(8,128)(2,1)S(1)}, u32[]{:S(2)}, u32[]{:S(2)}) collective-permute-start(bf16[592,128]{1,0:T(8,128)(2,1)S(1)} %pad_maximum_fusion.2), channel_id=1, source_target_pairs={{0,252},{4,0},{8,4},{12,8},{16,12},{20,16},{24,20},{28,24},{32,28}... | collective-permute-start | bytes 454664 | tf_op jit(solution)/shard_map/ppermute | solution.py:9
  17.0 0.6 collective-permute-start
  17.6 0.6 compare_and_fusion
  18.3 0.6 pad_clamp_fusion.1
  19.0 0.7 %copy.101 = pred[16,4]{1,0:T(8,128)(4,1)} copy(pred[16,4]{0,1:T(4,128)(4,1)S(1)} %get-tuple-element.7) | data formatting | bytes 128 | tf_op jit(solution)/shard_map/jit(_take)/and | solution.py:111
  19.9 0.6 pad_clamp_fusion.2
  20.6 6.6 %collective-permute-done = bf16[592,128]{1,0:T(8,128)(2,1)S(1)} collective-permute-done((bf16[592,128]{1,0:T(8,128)(2,1)S(1)}, bf16[592,128]{1,0:T(8,128)(2,1)S(1)}, u32[]{:S(2)}, u32[]{:S(2)}) %collective-permute-start) | collective-permute-done | bytes 151584 | tf_op jit(solution)/shard_map/ppermute | solution.py:9
  27.3 1.5 %collective-permute-start.4 = (bf16[64,128]{1,0:T(8,128)(2,1)S(1)}, bf16[64,128]{1,0:T(8,128)(2,1)}, u32[]{:S(2)}, u32[]{:S(2)}) collective-permute-start(bf16[64,128]{1,0:T(8,128)(2,1)S(1)} %bitcast.182), channel_id=1, source_target_pairs={{0,64},{4,68},{8,72},{12,76},{16,80},{20,84},{24,88},{28,92},{32,9... | collective-permute-start | bytes 49160 | tf_op jit(solution)/shard_map/ppermute | solution.py:9
  29.7 0.8 %gather_fusion.2 = bf16[16,8,2,256]{3,2,1,0:T(2,128)(2,1)S(1)} fusion(bf16[48,8,2,256]{3,2,1,0:T(2,128)(2,1)S(1)} %pad_maximum_fusion, s32[1024]{0:T(1024)S(1)} %pad_clamp_fusion), kind=kCustom, calls=%fused_computation.2 | custom fusion | bytes 262208 | tf_op jit(solution)/shard_map/jit(_take)/gather | solution.py:68
  30.7 3.4 %fusion.8 = f32[16,8,2,2,256]{4,1,2,3,0:T(8,128)S(1)} fusion(bf16[16,1,2,256,256]{4,3,2,1,0:T(8,128)(2,1)} %param.10, bf16[16,8,2,256,1]{3,2,1,0,4:T(2,128)(2,1)S(1)} %fusion.28), kind=kOutput, calls=%fused_computation.11 | convolution fusion | flops 67108864 | bytes 4849664 | tf_op jit(solution)/shard_map/lmapq,lmrcq->lracp/dot_general | solution.py:70
  34.2 0.6 %fusion.31 = bf16[16,4,2,256]{3,0,2,1:T(8,128)(2,1)} fusion(s32[]{:T(128)S(6)} %select_n.112, f32[16,2,4,1,256]{4,0,3,2,1:T(8,128)S(1)} %bitcast.166, f32[16,2,4,1,256]{4,0,3,2,1:T(8,128)S(1)} %bitcast.168), kind=kLoop, calls=%fused_computation.39 | loop fusion | flops 32768 | bytes 327684 | tf_op jit(solution)/shard_map/convert_element_type | solution.py:91
  34.9 4.2 %collective-permute-start.9 = (bf16[16,4,2,256]{3,0,2,1:T(8,128)(2,1)}, bf16[16,4,2,256]{3,0,2,1:T(8,128)(2,1)}, u32[]{:S(2)}, u32[]{:S(2)}) collective-permute-start(bf16[16,4,2,256]{3,0,2,1:T(8,128)(2,1)} %fusion.31), channel_id=1, source_target_pairs={{0,2},{1,3},{2,0},{3,1},{4,6},{5,7},{6,4},{7,5},{8,10},{9,11},{10,... | collective-permute-start | bytes 196616 | tf_op jit(solution)/shard_map/ppermute | solution.py:14
  39.1 0.6 copy-done.5
  39.7 1.4 %fusion.71 = (bf16[1,4,64,128]{3,2,1,0:T(8,128)(2,1)S(1)}, bf16[4,64,128]{2,1,0:T(8,128)(2,1)}) fusion(bf16[1,64,128]{2,1,0:T(8,128)(2,1)S(1)} %get-tuple-element.26, bf16[1,64,128]{2,1,0:T(8,128)(2,1)} %bitcast.199, bf16[1,64,128]{2,1,0:T(8,128)(2,1)S(1)} %bitcast.183, bf16[1,64,128]{2,1,0:T(8,128)(2,1)} %bitcast.39), kind=kLoop, calls=%fused_computation.143 | loop fusion | flops 98304 | bytes 196608 | tf_op jit(solution)/shard_map/stack | solution.py:85
  41.1 1.5 %collective-permute-start.6 = (bf16[4,64,128]{2,1,0:T(8,128)(2,1)}, bf16[4,64,128]{2,1,0:T(8,128)(2,1)}, u32[]{:S(2)}, u32[]{:S(2)}) collective-permute-start(bf16[4,64,128]{2,1,0:T(8,128)(2,1)} %get-tuple-element.20), channel_id=1, source_target_pairs={{0,16},{4,20},{8,24},{12,28},{16,32},{20,36},{24,40},{28,44},{32,4... | collective-permute-start | bytes 196616 | tf_op jit(solution)/shard_map/ppermute | solution.py:9
  42.7 1.5 %gather_fusion = bf16[64,2,2,128]{3,1,2,0:T(2,128)(2,1)} fusion(bf16[64,2,2,128]{3,1,0,2:T(2,128)(2,1)S(1)} %pad_maximum_fusion.3, s32[1024]{0:T(1024)} %pad_clamp_fusion.2), kind=kCustom, calls=%fused_computation | custom fusion | bytes 131328 | tf_op jit(solution)/shard_map/jit(_take)/gather | solution.py:111
  44.1 3.5 %fusion.17 = f32[16,2,2,2,128]{4,2,3,1,0:T(2,128)S(1)} fusion(pred[16,4]{1,0:T(8,128)(4,1)} %copy.101, bf16[16,4,2,2,128]{4,2,3,1,0:T(2,128)(2,1)} %bitcast.190, bf16[16,4,2,128,128]{4,3,2,1,0:T(8,128)(2,1)} %param.13), kind=kOutput, calls=%fused_computation.14 | convolution fusion | flops 16809984 | bytes 4325440 | tf_op jit(solution)/shard_map/lmakj,lmrcj->lrack/dot_general | solution.py:113
  47.6 0.6 fusion.43
  48.2 0.9 %fusion.26 = f32[16,4,2,256]{3,0,2,1:T(8,128)S(1)} fusion(s32[]{:T(128)S(6)} %select_n.111, f32[16,2,4,1,256]{4,0,3,2,1:T(8,128)S(1)} %bitcast.169, f32[16,2,4,1,256]{4,0,3,2,1:T(8,128)S(1)} %bitcast.167, bf16[16,4,2,256]{3,0,2,1:T(8,128)(2,1)} %collective-permute-done.9), kind=kLoop, calls=%fused_computation.32 | loop fusion | flops 98304 | bytes 458756 | tf_op jit(solution)/shard_map/add | solution.py:91
  49.1 0.6 %copy.196 = bf16[16,1,2,2,256]{4,3,2,0,1:T(2,128)(2,1)} copy(bf16[16,1,2,2,256]{4,0,3,2,1:T(8,128)(2,1)S(1)} %dynamic-slice_convert_fusion) | data formatting | bytes 65536
  49.8 3.9 %collective-permute-start.10 = (bf16[16,2,2,256]{3,2,1,0:T(2,128)(2,1)}, bf16[16,2,2,256]{3,2,1,0:T(2,128)(2,1)}, u32[]{:S(2)}, u32[]{:S(2)}) collective-permute-start(bf16[16,2,2,256]{3,2,1,0:T(2,128)(2,1)} %bitcast.165), channel_id=1, source_target_pairs={{0,1},{1,0},{2,3},{3,2},{4,5},{5,4},{6,7},{7,6},{8,9},{9,8},{10,11... | collective-permute-start | bytes 98312 | tf_op jit(solution)/shard_map/ppermute | solution.py:14
  53.7 0.9 %pad_maximum_fusion.1 = bf16[4,4,64,128]{3,2,1,0:T(8,128)(2,1)S(1)} fusion(bf16[1,4,64,128]{3,2,1,0:T(8,128)(2,1)} %bitcast.46, bf16[1,4,64,128]{3,2,1,0:T(8,128)(2,1)} %bitcast.45, bf16[1,4,64,128]{3,2,1,0:T(8,128)(2,1)S(1)} %get-tuple-element.19, bf16[1,4,64,128]{3,2,1,0:T(8,128)(2,1)} %bitcast.43), kind=kLoop, calls=%fused_computation.25 | loop fusion | flops 393216 | bytes 524288 | tf_op jit(solution)/shard_map/stack | solution.py:85
  54.7 0.7 %gather_fusion.1 = bf16[16,2,2,128]{3,2,1,0:T(2,128)(2,1)S(1)} fusion(bf16[256,2,2,128]{3,2,1,0:T(2,128)(2,1)S(1)} %bitcast.174, s32[1024]{0:T(1024)} %pad_clamp_fusion.1), kind=kCustom, calls=%fused_computation.1 | custom fusion | bytes 32832 | tf_op jit(solution)/shard_map/jit(_take)/gather | solution.py:118
  55.4 0.7 %select_bitcast_fusion = bf16[4,4,2,2,128,1]{4,1,0,3,2,5:T(4,128)(2,1)S(1)} fusion(bf16[4,4,2,2,128]{4,1,0,3,2:T(4,128)(2,1)S(1)} %bitcast.191, pred[4,4]{1,0:T(4,128)(4,1)} %get-tuple-element.9), kind=kLoop, calls=%fused_computation.77 | loop fusion | flops 8192 | bytes 32784 | tf_op jit(solution)/shard_map/jit(_take)/select_n | solution.py:118
  56.1 1.6 %convolution_bitcast_fusion.1 = f32[4,2,2,2,128]{4,3,2,1,0:T(2,128)S(1)} fusion(bf16[4,4,2,2,128,1]{4,1,0,3,2,5:T(4,128)(2,1)S(1)} %select_bitcast_fusion, bf16[4,4,2,128,128]{4,3,2,1,0:T(8,128)(2,1)} %param.16), kind=kOutput, calls=%fused_computation.16 | convolution fusion | flops 4194304 | bytes 1081344 | tf_op jit(solution)/shard_map/tmaqs,tmrcs->tracq/dot_general | solution.py:120
  58.2 0.7 %fusion.41 = bf16[16,2,2,128,1]{3,0,2,1,4:T(8,128)(2,1)S(1)} fusion(f32[16,2,1,128]{3,0,2,1:T(8,128)S(1)} %bitcast.189, f32[16,2,1,128]{3,0,2,1:T(8,128)S(1)} %bitcast.188, f32[16,2,1,128]{3,0,2,1:T(8,128)} %get-tuple-element.16, f32[16,2,1,128]{3,0,2,1:T(8,128)S(1)} %get-tuple-element.15), kind=kLoop, calls=%fused_computation.62 | loop fusion | flops 32768 | bytes 81920 | tf_op jit(solution)/shard_map/convert_element_type | solution.py:127
  59.5 1.5 %fusion.32 = bf16[16,2,2,256]{3,2,1,0:T(2,128)(2,1)} fusion(f32[16,2,1,256]{3,2,1,0:T(1,128)S(1)} %fusion.34, f32[16,2,1,256]{3,2,1,0:T(1,128)S(1)} %fusion.36, f32[16,1,2,2,256]{4,0,3,2,1:T(8,128)S(1)} %constant_dynamic-slice_fusion, bf16[16,2,2,256]{3,2,1,0:T(2,128)(2,1)} %collective-permute-done.10), kind=kLoop, calls=%fused_computation.43 | loop fusion | flops 81920 | bytes 196608 | tf_op jit(solution)/shard_map/convert_element_type | solution.py:131
  (84 shorter events, 3.2 us)
Async XLA Ops:
  0.0 1.6 %copy-start = (bf16[16,2,128,256]{3,2,1,0:T(8,128)(2,1)S(1)}, bf16[16,2,128,256]{3,2,1,0:T(8,128)(2,1)}, u32[]{:S(2)}) copy-start(bf16[16,2,128,256]{3,2,1,0:T(8,128)(2,1)} %param.12) | copy-start | bytes 6291460
  0.0 29.1 %copy-start.2 = (bf16[16,8,2,256]{3,2,1,0:T(2,128)(2,1)S(1)}, bf16[16,8,2,256]{3,2,1,0:T(2,128)(2,1)}, u32[]{:S(2)}) copy-start(bf16[16,8,2,256]{3,2,1,0:T(2,128)(2,1)} %param.9) | copy-start | bytes 393220
  0.0 17.6 %copy-start.8 = (s32[16,1]{0,1:T(1,128)S(1)}, s32[16,1]{0,1:T(1,128)}, u32[]{:S(2)}) copy-start(s32[16,1]{0,1:T(1,128)} %param.11) | copy-start | bytes 196
  0.0 17.6 %copy-start.7 = (s32[4,4]{1,0:T(4,128)S(1)}, s32[4,4]{1,0:T(4,128)}, u32[]{:S(2)}) copy-start(s32[4,4]{1,0:T(4,128)} %param.17) | copy-start | bytes 196
  0.0 18.8 %copy-start.6 = (s32[16,4]{0,1:T(4,128)S(1)}, s32[16,4]{0,1:T(4,128)}, u32[]{:S(2)}) copy-start(s32[16,4]{0,1:T(4,128)} %param.14) | copy-start | bytes 772
  4.8 22.4 %collective-permute-start.2 = (bf16[16,128]{1,0:T(8,128)(2,1)S(1)}, bf16[16,128]{1,0:T(8,128)(2,1)S(1)}, u32[]{:S(2)}, u32[]{:S(2)}) collective-permute-start(bf16[16,128]{1,0:T(8,128)(2,1)S(1)} %bitcast.194), channel_id=1, source_target_pairs={{0,248},{4,252},{8,0},{12,4},{16,8},{20,12},{24,16},{28,20},{32,24... | collective-permute-start | bytes 12296 | tf_op jit(solution)/shard_map/ppermute | solution.py:9
  16.0 4.6 %collective-permute-start.1 = (bf16[592,128]{1,0:T(8,128)(2,1)S(1)}, bf16[592,128]{1,0:T(8,128)(2,1)S(1)}, u32[]{:S(2)}, u32[]{:S(2)}) collective-permute-start(bf16[592,128]{1,0:T(8,128)(2,1)S(1)} %pad_maximum_fusion.2), channel_id=1, source_target_pairs={{0,252},{4,0},{8,4},{12,8},{16,12},{20,16},{24,20},{28,24},{32,28}... | collective-permute-start | bytes 454664 | tf_op jit(solution)/shard_map/ppermute | solution.py:9
  17.0 10.2 %collective-permute-start = (bf16[592,128]{1,0:T(8,128)(2,1)S(1)}, bf16[592,128]{1,0:T(8,128)(2,1)S(1)}, u32[]{:S(2)}, u32[]{:S(2)}) collective-permute-start(bf16[592,128]{1,0:T(8,128)(2,1)S(1)} %pad_maximum_fusion.2), channel_id=1, source_target_pairs={{0,4},{4,8},{8,12},{12,16},{16,20},{20,24},{24,28},{28,32},{32,36}... | collective-permute-start | bytes 454664 | tf_op jit(solution)/shard_map/ppermute | solution.py:9
  20.6 8.4 %copy-start.3 = (bf16[592,128]{1,0:T(8,128)(2,1)}, bf16[592,128]{1,0:T(8,128)(2,1)S(1)}, u32[]{:S(2)}) copy-start(bf16[592,128]{1,0:T(8,128)(2,1)S(1)} %collective-permute-done.1) | copy-start | bytes 454660
  27.2 1.7 %copy-start.4 = (bf16[592,128]{1,0:T(8,128)(2,1)}, bf16[592,128]{1,0:T(8,128)(2,1)S(1)}, u32[]{:S(2)}) copy-start(bf16[592,128]{1,0:T(8,128)(2,1)S(1)} %collective-permute-done) | copy-start | bytes 454660
  27.2 11.9 %collective-permute-start.5 = (bf16[64,128]{1,0:T(8,128)(2,1)S(1)}, bf16[64,128]{1,0:T(8,128)(2,1)S(1)}, u32[]{:S(2)}, u32[]{:S(2)}) collective-permute-start(bf16[64,128]{1,0:T(8,128)(2,1)S(1)} %bitcast.181), channel_id=1, source_target_pairs={{0,192},{4,196},{8,200},{12,204},{16,208},{20,212},{24,216},{28,22... | collective-permute-start | bytes 49160 | tf_op jit(solution)/shard_map/ppermute | solution.py:9
  27.3 11.8 %collective-permute-start.4 = (bf16[64,128]{1,0:T(8,128)(2,1)S(1)}, bf16[64,128]{1,0:T(8,128)(2,1)}, u32[]{:S(2)}, u32[]{:S(2)}) collective-permute-start(bf16[64,128]{1,0:T(8,128)(2,1)S(1)} %bitcast.182), channel_id=1, source_target_pairs={{0,64},{4,68},{8,72},{12,76},{16,80},{20,84},{24,88},{28,92},{32,9... | collective-permute-start | bytes 49160 | tf_op jit(solution)/shard_map/ppermute | solution.py:9
  28.9 6.0 %slice-start.1 = ((bf16[592,128]{1,0:T(8,128)(2,1)}), bf16[64,128]{1,0:T(8,128)(2,1)S(1)}, s32[]{:S(2)}) async-start(bf16[592,128]{1,0:T(8,128)(2,1)} %copy-done.4), calls=%async_computation.1 | async-start | bytes 32768 | tf_op jit(solution)/shard_map/slice | solution.py:101
  29.0 10.1 %collective-permute-start.3 = (bf16[128,128]{1,0:T(8,128)(2,1)S(1)}, bf16[128,128]{1,0:T(8,128)(2,1)S(1)}, u32[]{:S(2)}, u32[]{:S(2)}) collective-permute-start(bf16[128,128]{1,0:T(8,128)(2,1)S(1)} %pad_maximum_fusion.5), channel_id=1, source_target_pairs={{0,128},{4,132},{8,136},{12,140},{16,144},{20,148},{24,152},{28,15... | collective-permute-start | bytes 98312 | tf_op jit(solution)/shard_map/ppermute | solution.py:9
  29.1 5.7 %slice-start = ((bf16[592,128]{1,0:T(8,128)(2,1)}), bf16[64,128]{1,0:T(8,128)(2,1)S(1)}, s32[]{:S(2)}) async-start(bf16[592,128]{1,0:T(8,128)(2,1)} %copy-done.3), calls=%async_computation | async-start | bytes 32768 | tf_op jit(solution)/shard_map/slice | solution.py:103
  34.9 22.9 %copy-start.1 = (bf16[16,2,128,128]{3,2,1,0:T(8,128)(2,1)S(1)}, bf16[16,2,128,128]{3,2,1,0:T(8,128)(2,1)}, u32[]{:S(2)}) copy-start(bf16[16,2,128,128]{3,2,1,0:T(8,128)(2,1)} %param.15) | copy-start | bytes 3145732
  34.9 13.3 %collective-permute-start.9 = (bf16[16,4,2,256]{3,0,2,1:T(8,128)(2,1)}, bf16[16,4,2,256]{3,0,2,1:T(8,128)(2,1)}, u32[]{:S(2)}, u32[]{:S(2)}) collective-permute-start(bf16[16,4,2,256]{3,0,2,1:T(8,128)(2,1)} %fusion.31), channel_id=1, source_target_pairs={{0,2},{1,3},{2,0},{3,1},{4,6},{5,7},{6,4},{7,5},{8,10},{9,11},{10,... | collective-permute-start | bytes 196616 | tf_op jit(solution)/shard_map/ppermute | solution.py:14
  39.1 0.6 copy-start.5
  41.1 12.6 %collective-permute-start.7 = (bf16[4,64,128]{2,1,0:T(8,128)(2,1)}, bf16[4,64,128]{2,1,0:T(8,128)(2,1)}, u32[]{:S(2)}, u32[]{:S(2)}) collective-permute-start(bf16[4,64,128]{2,1,0:T(8,128)(2,1)} %get-tuple-element.20), channel_id=1, source_target_pairs={{0,240},{4,244},{8,248},{12,252},{16,0},{20,4},{24,8},{28,12},{32,... | collective-permute-start | bytes 196616 | tf_op jit(solution)/shard_map/ppermute | solution.py:9
  41.1 12.6 %collective-permute-start.8 = (bf16[4,64,128]{2,1,0:T(8,128)(2,1)}, bf16[4,64,128]{2,1,0:T(8,128)(2,1)}, u32[]{:S(2)}, u32[]{:S(2)}) collective-permute-start(bf16[4,64,128]{2,1,0:T(8,128)(2,1)} %get-tuple-element.20), channel_id=1, source_target_pairs={{0,224},{4,228},{8,232},{12,236},{16,240},{20,244},{24,248},{28,25... | collective-permute-start | bytes 196616 | tf_op jit(solution)/shard_map/ppermute | solution.py:9
  41.1 12.6 %collective-permute-start.6 = (bf16[4,64,128]{2,1,0:T(8,128)(2,1)}, bf16[4,64,128]{2,1,0:T(8,128)(2,1)}, u32[]{:S(2)}, u32[]{:S(2)}) collective-permute-start(bf16[4,64,128]{2,1,0:T(8,128)(2,1)} %get-tuple-element.20), channel_id=1, source_target_pairs={{0,16},{4,20},{8,24},{12,28},{16,32},{20,36},{24,40},{28,44},{32,4... | collective-permute-start | bytes 196616 | tf_op jit(solution)/shard_map/ppermute | solution.py:9
  49.8 9.7 %collective-permute-start.10 = (bf16[16,2,2,256]{3,2,1,0:T(2,128)(2,1)}, bf16[16,2,2,256]{3,2,1,0:T(2,128)(2,1)}, u32[]{:S(2)}, u32[]{:S(2)}) collective-permute-start(bf16[16,2,2,256]{3,2,1,0:T(2,128)(2,1)} %bitcast.165), channel_id=1, source_target_pairs={{0,1},{1,0},{2,3},{3,2},{4,5},{5,4},{6,7},{7,6},{8,9},{9,8},{10,11... | collective-permute-start | bytes 98312 | tf_op jit(solution)/shard_map/ppermute | solution.py:14

commit v2 on v0

v2 whole, which is shorter than its diff:
```python
import functools

import jax
import jax.numpy as jnp
from jax import lax
from jax.experimental import pallas as pl
from jax.experimental.pallas import tpu as pltpu
from jax.sharding import PartitionSpec as P

F32 = jnp.float32
BF16 = jnp.bfloat16
ALONG_LAST = (((1,), (1,)), ((), ()))
ALONG_ROWS = (((1,), (0,)), ((), ()))


def dot(left, right, dims):
    return lax.dot_general(left, right, dims, preferred_element_type=F32)


def turned(value):
    rows = value.shape[0]
    even = lax.broadcasted_iota(jnp.int32, value.shape, 0) % 2 == 0
    return jnp.where(even, -pltpu.roll(value, rows - 1, 0), pltpu.roll(value, 1, 0))


def complex_rows(value):
    half = value.shape[1] // 2
    return value[:, :half] + turned(value[:, half:])


class Stream:
    def __init__(self, pairs, arrived, ahead):
        self.copies = [
            pltpu.make_async_copy(source, target, arrived.at[i])
            for i, (source, target) in enumerate(pairs)
        ]
        self.ahead = ahead
        for copy in self.copies[:ahead]:
            copy.start()

    def wait(self, index):
        self.copies[index].wait()
        if index + self.ahead < len(self.copies):
            self.copies[index + self.ahead].start()


def up_kernel(
    leaves, top_dev, own, charges_hbm, basis_hbm, transfer_hbm, parents, coefs, message,
    charges, basis, transfer, coef, rows, own_coef, own_parent, arrived,
):
    rank = basis.shape[2]
    branch = leaves // top_dev
    parts = [pl.ds(top * branch, branch) for top in range(top_dev)]
    stream = Stream(
        [(charges_hbm, charges)]
        + [(basis_hbm.at[part], basis.at[part]) for part in parts]
        + [(transfer_hbm.at[part], transfer.at[part]) for part in parts],
        arrived,
        1 + 2 * top_dev,
    )
    count = charges.shape[1] * 2
    first = pl.multiple_of(lax.axis_index("rhs") * own, own)
    coef_rows = leaves * own
    stream.wait(0)
    for leaf in range(leaves):
        if leaf % branch == 0:
            stream.wait(1 + leaf // branch)
        source = charges[leaf].reshape(count, charges.shape[3])
        product = dot(source, basis[leaf].reshape(2 * rank, -1), ALONG_LAST)
        coef[leaf] = complex_rows(product)
        own_coef[own * leaf : own * (leaf + 1), :] = coef[leaf, pl.ds(first, own), :]
        start = coef_rows + 2 * count * leaf
        message[start : start + count, :] = source[:, :rank]
        message[start + count : start + 2 * count, :] = source[:, rank:]
    coefs[...] = own_coef[...].astype(BF16)
    message[:coef_rows, :] = own_coef[...].astype(BF16)
    for top in range(top_dev):
        stream.wait(1 + top_dev + top)
        total = jnp.zeros((count, rank), F32)
        for leaf in range(top * branch, (top + 1) * branch):
            value = coef[leaf].astype(BF16).astype(F32)
            pair = jnp.concatenate([value, turned(value)], axis=1).astype(BF16)
            total += dot(pair, transfer[leaf].reshape(2 * rank, -1), ALONG_ROWS)
        rows[...] = total
        own_parent[own * top : own * (top + 1), :] = rows[pl.ds(first, own), :]
    parents[...] = jnp.broadcast_to(own_parent[...].astype(BF16)[None], parents.shape)


def near_kernel(
    leaves, own, near_hbm, places_hbm, message, even_side, odd_side, blocks_hbm, kept, sent, sources,
    near_list, places, blocks, table, coef_table, coef_wide, listed, tabled, arrived,
):
    points = blocks.shape[4]
    rank = message.shape[1]
    span = leaves * own
    size = message.shape[0] - span
    each = size // leaves
    count = each // 2
    lists = Stream([(near_hbm, near_list), (places_hbm, places)], listed, 2)
    me = lax.axis_index("leaf")
    order = ((even_side, 2 - 2 * (me % 2)), (message, 1), (odd_side, 2 * (me % 2)))
    tables = Stream(
        [
            (source.at[pl.ds(span, size)], table.at[pl.ds(pl.multiple_of(size * i, size), size)])
            for source, i in order
        ]
        + [
            (source.at[pl.ds(0, span)], coef_table.at[pl.ds(pl.multiple_of(span * i, span), span)])
            for source, i in order
        ],
        tabled,
        6,
    )
    step = 4
    chunks = [pl.ds(leaf, step) for leaf in range(0, leaves, step)]
    stream = Stream([(blocks_hbm.at[part], blocks.at[part]) for part in chunks], arrived, 4)
    first_leaf = me * leaves
    core = lax.axis_index("rhs") % 2
    for i in range(2):
        lists.wait(i)
    for i in range(6):
        tables.wait(i)
    others = []
    for leaf in range(leaves):
        place = (near_list[0, leaf] - first_leaf + leaves) * each
        value = table[pl.ds(pl.multiple_of(place, each), each), :]
        value = jnp.concatenate([value[:count], value[count:]], axis=1)
        if leaf % step == 0:
            stream.wait(leaf // step)
        product = dot(value, blocks[leaf, 0].reshape(2 * points, points), ALONG_LAST)
        value = complex_rows(product)
        for part in range(2):
            row = 2 * own * leaf + own * part
            first = value[2 * own * part : 2 * own * part + own]
            second = value[2 * own * part + own : 2 * own * (part + 1)]
            kept[row : row + own, :] = jnp.where(core == 0, first, second)
            others.append(jnp.where(core == 0, second, first))
    sent[...] = jnp.concatenate(others).astype(BF16)
    coef_wide[...] = coef_table[...].astype(F32)
    for leaf in range(leaves):
        for slot in range(1, places.shape[0]):
            place = pl.multiple_of((places[slot, leaf] - first_leaf + leaves) * own, own)
            sources[own * leaf : own * (leaf + 1), rank * (slot - 1) : rank * slot] = coef_wide[
                pl.ds(place, own), :
            ]


def coupling_kernel(leaves, own, distant, sources, coupling, field):
    rank = coupling.shape[4]
    for leaf in range(leaves):
        part = slice(own * leaf, own * (leaf + 1))
        value = jnp.concatenate([distant[part, :].astype(F32), sources[part, :]], axis=1)
        weights = jnp.concatenate(
            [coupling[leaf, slot].reshape(2 * rank, rank) for slot in range(coupling.shape[1])], axis=1
        )
        field[part, :] = complex_rows(dot(value.astype(BF16), weights, ALONG_LAST))


def sum_kernel(leaves, own, far, mine, received, product):
    for leaf in range(leaves):
        part = slice(own * leaf, own * (leaf + 1))
        value = far[part, :] + mine[part, :] + received[part, :].astype(F32)
        product[leaf] = value.astype(BF16).reshape(product.shape[1:])


def half_kernel(leaves, own, kept, received, mine, sent):
    part = lax.axis_index("rhs") // 2
    total = kept[...] + received[...].astype(F32)
    others = []
    for leaf in range(leaves):
        row = own * leaf
        first = total[2 * row : 2 * row + own]
        second = total[2 * row + own : 2 * row + 2 * own]
        mine[row : row + own, :] = jnp.where(part == 0, first, second)
        others.append(jnp.where(part == 0, second, first))
    sent[...] = jnp.concatenate(others).astype(BF16)


def down_kernel(
    leaves, own, tops_hbm, gathered, top_hbm, transfer, basis, field, result,
    tops, top_coupling, table, listed, arrived,
):
    rank = basis.shape[2]
    top_dev = top_coupling.shape[0]
    slots = top_coupling.shape[1]
    branch = leaves // top_dev
    lists = Stream([(tops_hbm, tops)], listed, 1)
    stream = Stream([(top_hbm.at[top], top_coupling.at[top]) for top in range(top_dev)], arrived, 4)
    table[...] = gathered[...].astype(F32).reshape(table.shape)
    lists.wait(0)
    for top in range(top_dev):
        values = []
        for slot in range(slots):
            values.append(table[pl.ds(pl.multiple_of(tops[top, slot] * own, own), own), :])
        value = jnp.concatenate(values, axis=1).astype(BF16)
        stream.wait(top)
        weights = jnp.concatenate(
            [top_coupling[top, slot].reshape(2 * rank, rank) for slot in range(slots)], axis=1
        )
        top_field = complex_rows(dot(value, weights, ALONG_LAST)).astype(BF16)
        for leaf in range(top * branch, (top + 1) * branch):
            down = complex_rows(dot(top_field, transfer[leaf].reshape(2 * rank, rank), ALONG_LAST))
            value = (down + field[own * leaf : own * (leaf + 1), :]).astype(BF16).astype(F32)
            pair = jnp.concatenate([value, turned(value)], axis=1).astype(BF16)
            result[own * leaf : own * (leaf + 1), :] = dot(
                pair, basis[leaf].reshape(2 * rank, -1), ALONG_ROWS
            )


VMEM = pl.BlockSpec(memory_space=pltpu.VMEM)
SMEM = pl.BlockSpec(memory_space=pltpu.SMEM)
HBM = pl.BlockSpec(memory_space=pltpu.HBM)
ANY = pl.BlockSpec(memory_space=pl.ANY)


def call(kernel, out_shape, scratch, ops, specs, flops, room):
    ops = [
        pltpu.with_memory_space_constraint(value, pltpu.HBM) if specs.get(i) is HBM else value
        for i, value in enumerate(ops)
    ]
    return pl.pallas_call(
        kernel,
        out_shape=[jax.ShapeDtypeStruct(*shape) for shape in out_shape],
        in_specs=[specs.get(i, VMEM) for i in range(len(ops))],
        out_specs=[VMEM] * len(out_shape),
        scratch_shapes=scratch,
        compiler_params=pltpu.CompilerParams(vmem_limit_bytes=room * 2**20),
        cost_estimate=pl.CostEstimate(flops=flops, bytes_accessed=4 * 2**20, transcendentals=0),
    )(*ops)


def shifted(value, axis, step):
    count = lax.axis_size(axis)
    return lax.ppermute(value, axis, [(i, (i - step) % count) for i in range(count)])


def paired(value, axis, first):
    count = lax.axis_size(axis)
    pairs = []
    for i in range(first, count - 1, 2):
        pairs += [(i, i + 1), (i + 1, i)]
    return lax.ppermute(value, axis, pairs)


def flipped(value, axis, bit):
    count = lax.axis_size(axis)
    return lax.ppermute(value, axis, [(i, i ^ bit) for i in range(count)])


def local(
    charges,
    near_blocks,
    near_list,
    basis,
    coupling,
    coupling_list,
    transfer,
    top_coupling,
    top_list,
):
    leaves, rhs_all, _, points = charges.shape
    rhs_dev = rhs_all // lax.axis_size("rhs")
    top_dev = top_coupling.shape[0]
    rank = basis.shape[2]
    groups = lax.axis_size("leaf")
    count, own = 2 * rhs_all, 2 * rhs_dev
    parent_rows, coef_rows = top_dev * own, leaves * own
    parents, coefs, message = call(
        functools.partial(up_kernel, leaves, top_dev, own),
        [
            ((groups, parent_rows, rank), BF16),
            ((coef_rows, rank), BF16),
            ((coef_rows + leaves * 2 * count, rank), BF16),
        ],
        [
            pltpu.VMEM(charges.shape, BF16),
            pltpu.VMEM(basis.shape, BF16),
            pltpu.VMEM(transfer.shape, BF16),
            pltpu.VMEM((leaves, count, rank), F32),
            pltpu.VMEM((count, rank), F32),
            pltpu.VMEM((coef_rows, rank), F32),
            pltpu.VMEM((parent_rows, rank), F32),
            pltpu.SemaphoreType.DMA((1 + 2 * top_dev,)),
        ],
        (charges, basis, transfer),
        {0: HBM, 1: HBM, 2: HBM},
        2 * 10**8,
        8,
    )
    gathered = lax.all_to_all(parents, "leaf", 0, 0, tiled=True)
    odd_side = paired(message, "leaf", 1)
    even_side = paired(message, "leaf", 0)
    distant = shifted(coefs, "leaf", groups // 2)
    kept, sent, sources = call(
        functools.partial(near_kernel, leaves, own),
        [
            ((leaves * 2 * own, points), F32),
            ((leaves * 2 * own, points), BF16),
            ((coef_rows, 3 * rank), F32),
        ],
        [
            pltpu.SMEM((1, leaves), jnp.int32),
            pltpu.SMEM((coupling_list.shape[1], leaves), jnp.int32),
            pltpu.VMEM(near_blocks.shape, BF16),
            pltpu.VMEM((3 * leaves * 2 * count, rank), BF16),
            pltpu.VMEM((3 * coef_rows, rank), BF16),
            pltpu.VMEM((3 * coef_rows, rank), F32),
            pltpu.SemaphoreType.DMA((2,)),
            pltpu.SemaphoreType.DMA((6,)),
            pltpu.SemaphoreType.DMA((leaves // 4,)),
        ],
        (near_list.T, coupling_list.T, message, even_side, odd_side, near_blocks),
        {0: HBM, 1: HBM, 2: ANY, 3: ANY, 4: ANY, 5: HBM},
        2 * 10**9,
        8,
    )
    received = flipped(sent, "rhs", 1)
    (field,) = call(
        functools.partial(coupling_kernel, leaves, own),
        [((coef_rows, rank), F32)],
        [],
        (distant, sources, coupling),
        {},
        2 * 10**9,
        6,
    )
    mine, sent = call(
        functools.partial(half_kernel, leaves, own),
        [((leaves * own, points), F32), ((leaves * own, points), BF16)],
        [],
        (kept, received),
        {},
        10**7,
        2,
    )
    received = flipped(sent, "rhs", 2)
    (far_part,) = call(
        functools.partial(down_kernel, leaves, own),
        [((leaves * own, points), F32)],
        [
            pltpu.SMEM(top_list.shape, jnp.int32),
            pltpu.VMEM(top_coupling.shape, BF16),
            pltpu.VMEM((groups * parent_rows, rank), F32),
            pltpu.SemaphoreType.DMA((1,)),
            pltpu.SemaphoreType.DMA((top_dev,)),
        ],
        (top_list, gathered, top_coupling, transfer, basis, field),
        {0: HBM, 2: HBM},
        2 * 10**9,
        6,
    )
    (product,) = call(
        functools.partial(sum_kernel, leaves, own),
        [((leaves, rhs_dev, 2, points), BF16)],
        [],
        (far_part, mine, received),
        {},
        10**7,
        2,
    )
    return product


def solution(mesh):
    return jax.shard_map(
        local,
        mesh=mesh,
        in_specs=(
            P("leaf", None, None, None),
            P("leaf", "rhs", None, None, None),
            P("leaf", "rhs"),
            P("leaf", None, None, None),
            P("leaf", None, None, None, None),
            P("leaf", None),
            P("leaf", None, None, None),
            P("leaf", None, None, None, None),
            P("leaf", None),
        ),
        out_specs=P("leaf", "rhs", None, None),
        check_vma=False,
    )
```

time: 381 us -> 39.5 us (0.10)
  blocking collectives: 183 us -> 0 us
  waiting for transfers between devices: 152 us -> 2.02 us
  starting transfers between devices: 6.16 us -> 23.6 us
  between operations: 15.1 us -> 0.13 us
  matrix products: 13 us -> 0 us
  Pallas kernels: 0 us -> 12.1 us
  other arithmetic: 5.73 us -> 0 us
  local copies, waits for them, and re-layouts: 5.81 us -> 1.34 us
    all_gather x1 -> x0, blocking collectives: 183 us -> none  [local(): fetched = lax.all_gather(parent_coef, 'leaf', axis=0, tiled=True)]
    all_gather x1 -> x0, waiting for transfers between devices: 152 us -> none  [local(): source_table = lax.all_gather(coefficients, 'leaf', axis=0, tiled=True)]
    dot_general x8 -> x0, matrix products: 13 us -> none  [the longest x1 3.41 us: local(): jnp.einsum('lmakj,lmrcj->lrack', coupling, sources, preferred_element_typ...]
    all_to_all x0 -> x1, starting transfers between devices: none -> 13 us  [local(): gathered = lax.all_to_all(parents, 'leaf', 0, 0, tiled=True)]
    pallas_call x0 -> x6, Pallas kernels: none -> 12.1 us  [call(): pl.pallas_call(kernel, out_shape=[jax.ShapeDtypeStruct(*shape) for shape...]
    ppermute x2 -> x5, starting transfers between devices: 6.11 us -> 10.6 us  [the longest x2 4.59 us: flipped(): return lax.ppermute(value, axis, [(i, i ^ bit) for i in range(count)])]
  transfers between devices with their start and end apart: 4 -> 6, of which waited for: 1 -> 1; matrix products, arithmetic and copies ran while one was open for 6% -> 0% of each run, Pallas kernels for 0% -> 20%
where the time goes in v2:
time: 39.5 us; the launch traced here: 39.2 us
  starting transfers between devices  23.6 us (60%)
  Pallas kernels  12.1 us (31%)
  waiting for transfers between devices  2.02 us (5%)
  local copies, waits for them, and re-layouts  1.34 us (3%)
    all_to_all x1, starting transfers between devices, local(): gathered = lax.all_to_all(parents, 'leaf', 0, 0, tiled=True)  13 us
    pallas_call x6, Pallas kernels, call(): pl.pallas_call(kernel, out_shape=[jax.ShapeDtypeStruct(*shape) for shape...  12.1 us
    ppermute x2, starting transfers between devices, flipped(): return lax.ppermute(value, axis, [(i, i ^ bit) for i in range(count)])  4.59 us
    ppermute x2, starting transfers between devices, paired(): return lax.ppermute(value, axis, pairs)  3.49 us
    ppermute x1, starting transfers between devices, shifted(): lax.ppermute(value, axis, [(i, (i - step) % count) for i in range(count)])  2.55 us
    ppermute x1, waiting for transfers between devices, shifted(): lax.ppermute(value, axis, [(i, (i - step) % count) for i in range(count)])  2 us
    unnamed x10, local copies, waits for them, and re-layouts  1.34 us
  transfers between devices with their start and end apart: 6, of which 1 were waited for; matrix products, arithmetic and copies ran while one was open for 0% of the time, Pallas kernels for 20%

profile of v2, /device:TPU:2, one launch (start us, length us, event | category | flops | bytes accessed | tf_op | source)
XLA Modules:
  0.0 39.2 jit_solution(2036872193482436027)
XLA Ops:
  0.0 3.6 %shard_map.91 = (bf16[64,16,128]{2,1,0:T(8,128)(2,1)}, bf16[64,128]{1,0:T(8,128)(2,1)S(1)}, bf16[576,128]{1,0:T(8,128)(2,1)S(1)}) custom-call(bf16[16,8,2,256]{3,2,1,0:T(2,128)(2,1)} %charges_hbm.1, bf16[16,2,128,256]{3,2,1,0:T(8,128)(2,1)} %basis.1, bf16[16,2,128,128]{3,2,1,0:T(8,128)(2,1)} %transfer.1), custom_call_target="tpu_custom_call" | custom-call | flops 200000000 | bytes 4194304 | tf_op jit(solution)/shard_map/pallas_call | solution.py:221
  3.6 3.4 %collective-permute-start.2 = (bf16[576,128]{1,0:T(8,128)(2,1)S(1)}, bf16[576,128]{1,0:T(8,128)(2,1)S(1)}, u32[]{:S(2)}, u32[]{:S(2)}) collective-permute-start(bf16[576,128]{1,0:T(8,128)(2,1)S(1)} %get-tuple-element.15.message), channel_id=1, source_target_pairs={{4,8},{8,4},{12,16},{16,12},{20,24},{24,20},{28,32},{32,28},{36,40... | collective-permute-start | bytes 442376 | tf_op jit(solution)/shard_map/ppermute | solution.py:242
  7.0 0.1 collective-permute-start.1
  7.1 13.0 %all-to-all-start = ((bf16[64,16,128]{2,1,0:T(8,128)(2,1)}), bf16[64,16,128]{2,1,0:T(8,128)(2,1)S(1)}, u32[]{:S(2)}, u32[]{:S(2)}) async-start(bf16[64,16,128]{2,1,0:T(8,128)(2,1)} %get-tuple-element.13), calls=%async_computation | async-start | bytes 524288 | tf_op jit(solution)/shard_map/all_to_all | solution.py:290
  20.1 0.0 copy-start.2
  20.1 2.6 %collective-permute-start = (bf16[64,128]{1,0:T(8,128)(2,1)S(1)}, bf16[64,128]{1,0:T(8,128)(2,1)S(1)}, u32[]{:S(2)}, u32[]{:S(2)}) collective-permute-start(bf16[64,128]{1,0:T(8,128)(2,1)S(1)} %get-tuple-element.14), channel_id=1, source_target_pairs={{0,128},{4,132},{8,136},{12,140},{16,144},{20,148},{24,152},{28,15... | collective-permute-start | bytes 49160 | tf_op jit(solution)/shard_map/ppermute | solution.py:234
  22.7 0.0 collective-permute-done.2.odd_side
  22.7 0.0 collective-permute-done.1.even_side
  22.7 3.5 %shard_map.92 = (f32[128,256]{1,0:T(8,128)S(1)}, bf16[128,256]{1,0:T(8,128)(2,1)S(1)}, f32[64,384]{1,0:T(8,128)S(1)}) custom-call(s32[1,16]{1,0:T(1,128)} %bitcast.3, s32[4,16]{1,0:T(4,128)} %bitcast.2, bf16[576,128]{1,0:T(8,128)(2,1)S(1)} %get-tuple-element.15.message, bf16[576,128]{1,0:T(8,128)(2,1)S(1)} %collective-permute-done.1.even_side, ...), custom_call_target="tpu_custom_call" | custom-call | flops 2000000000 | bytes 4194304 | tf_op jit(solution)/shard_map/pallas_call | solution.py:221
  26.2 0.0 copy-start
  26.2 0.0 copy-start.1
  26.2 0.1 collective-permute-start.3
  26.3 2.0 %collective-permute-done.distant = bf16[64,128]{1,0:T(8,128)(2,1)S(1)} collective-permute-done((bf16[64,128]{1,0:T(8,128)(2,1)S(1)}, bf16[64,128]{1,0:T(8,128)(2,1)S(1)}, u32[]{:S(2)}, u32[]{:S(2)}) %collective-permute-start) | collective-permute-done | bytes 16416 | tf_op jit(solution)/shard_map/ppermute | solution.py:234
  28.3 0.0 copy-done.2
  28.3 1.2 %shard_map.93.field = f32[64,128]{1,0:T(8,128)S(1)} custom-call(bf16[64,128]{1,0:T(8,128)(2,1)S(1)} %collective-permute-done.distant, f32[64,384]{1,0:T(8,128)S(1)} %get-tuple-element.16.sources, bf16[16,4,2,128,128]{4,3,2,1,0:T(8,128)(2,1)S(1)} %copy-done.2), custom_call_target="tpu_custom_call" | custom-call | flops 2000000000 | bytes 4194304 | tf_op jit(solution)/shard_map/pallas_call | solution.py:221
  29.5 0.0 copy-start.3
  29.5 0.0 collective-permute-done.3.received
  29.6 0.6 %copy-done.3 = f32[64,128]{1,0:T(8,128)} copy-done((f32[64,128]{1,0:T(8,128)}, f32[64,128]{1,0:T(8,128)S(1)}, u32[]{:S(2)}) %copy-start.3) | copy-done | bytes 32792
  30.1 4.5 %collective-permute-start.4 = (bf16[64,256]{1,0:T(8,128)(2,1)S(1)}, bf16[64,256]{1,0:T(8,128)(2,1)S(1)}, u32[]{:S(2)}, u32[]{:S(2)}) collective-permute-start(bf16[64,256]{1,0:T(8,128)(2,1)S(1)} %get-tuple-element.20), channel_id=1, source_target_pairs={{0,2},{1,3},{2,0},{3,1},{4,6},{5,7},{6,4},{7,5},{8,10},{9,11},{10,... | collective-permute-start | bytes 98312 | tf_op jit(solution)/shard_map/ppermute | solution.py:247
  34.6 0.0 all-to-all-done.gathered
  34.6 0.0 copy-done
  34.6 0.0 copy-done.1
  34.6 0.0 copy-start.4
  34.7 0.7 %copy-done.4 = f32[64,128]{1,0:T(8,128)S(1)} copy-done((f32[64,128]{1,0:T(8,128)S(1)}, f32[64,128]{1,0:T(8,128)}, u32[]{:S(2)}) %copy-start.4) | copy-done | bytes 32792
  35.4 3.2 %shard_map.94.far = f32[64,256]{1,0:T(8,128)S(1)} custom-call(s32[4,4]{1,0:T(4,128)} %tops_hbm.1, bf16[64,16,128]{2,1,0:T(8,128)(2,1)S(1)} %all-to-all-done.gathered, bf16[4,4,2,128,128]{4,3,2,1,0:T(8,128)(2,1)} %top_hbm.1, bf16[16,2,128,128]{3,2,1,0:T(8,128)(2,1)S(1)} %copy-done.1, bf16[16,2,128,256]{3,2,1,0:T(8,128)(2,1)S(1)} %copy-done, ...), custom_call_target="tpu_custom_call" | custom-call | flops 2000000000 | bytes 4194304 | tf_op jit(solution)/shard_map/pallas_call | solution.py:221
  38.6 0.0 collective-permute-done.4.received
  38.6 0.6 %shard_map.96 = bf16[16,2,2,256]{3,2,1,0:T(2,128)(2,1)} custom-call(f32[64,256]{1,0:T(8,128)S(1)} %shard_map.94.far, f32[64,256]{1,0:T(8,128)S(1)} %get-tuple-element.19.mine, bf16[64,256]{1,0:T(8,128)(2,1)S(1)} %collective-permute-done.4.received), custom_call_target="tpu_custom_call" | custom-call | flops 10000000 | bytes 4194304 | tf_op jit(solution)/shard_map/pallas_call | solution.py:221
  (1 shorter events, 0.0 us)
Async XLA Ops:
  3.6 19.1 %collective-permute-start.2 = (bf16[576,128]{1,0:T(8,128)(2,1)S(1)}, bf16[576,128]{1,0:T(8,128)(2,1)S(1)}, u32[]{:S(2)}, u32[]{:S(2)}) collective-permute-start(bf16[576,128]{1,0:T(8,128)(2,1)S(1)} %get-tuple-element.15.message), channel_id=1, source_target_pairs={{4,8},{8,4},{12,16},{16,12},{20,24},{24,20},{28,32},{32,28},{36,40... | collective-permute-start | bytes 442376 | tf_op jit(solution)/shard_map/ppermute | solution.py:242
  7.0 15.7 %collective-permute-start.1 = (bf16[576,128]{1,0:T(8,128)(2,1)S(1)}, bf16[576,128]{1,0:T(8,128)(2,1)S(1)}, u32[]{:S(2)}, u32[]{:S(2)}) collective-permute-start(bf16[576,128]{1,0:T(8,128)(2,1)S(1)} %get-tuple-element.15.message), channel_id=1, source_target_pairs={{0,4},{4,0},{8,12},{12,8},{16,20},{20,16},{24,28},{28,24},{32,36},... | collective-permute-start | bytes 442376 | tf_op jit(solution)/shard_map/ppermute | solution.py:242
  7.1 27.5 %all-to-all-start = ((bf16[64,16,128]{2,1,0:T(8,128)(2,1)}), bf16[64,16,128]{2,1,0:T(8,128)(2,1)S(1)}, u32[]{:S(2)}, u32[]{:S(2)}) async-start(bf16[64,16,128]{2,1,0:T(8,128)(2,1)} %get-tuple-element.13), calls=%async_computation | async-start | bytes 524288 | tf_op jit(solution)/shard_map/all_to_all | solution.py:290
  20.1 8.2 %copy-start.2 = (bf16[16,4,2,128,128]{4,3,2,1,0:T(8,128)(2,1)S(1)}, bf16[16,4,2,128,128]{4,3,2,1,0:T(8,128)(2,1)}, u32[]{:S(2)}) copy-start(bf16[16,4,2,128,128]{4,3,2,1,0:T(8,128)(2,1)} %coupling.1) | copy-start | bytes 12582916
  20.1 8.2 %collective-permute-start = (bf16[64,128]{1,0:T(8,128)(2,1)S(1)}, bf16[64,128]{1,0:T(8,128)(2,1)S(1)}, u32[]{:S(2)}, u32[]{:S(2)}) collective-permute-start(bf16[64,128]{1,0:T(8,128)(2,1)S(1)} %get-tuple-element.14), channel_id=1, source_target_pairs={{0,128},{4,132},{8,136},{12,140},{16,144},{20,148},{24,152},{28,15... | collective-permute-start | bytes 49160 | tf_op jit(solution)/shard_map/ppermute | solution.py:234
  26.2 8.5 %copy-start = (bf16[16,2,128,256]{3,2,1,0:T(8,128)(2,1)S(1)}, bf16[16,2,128,256]{3,2,1,0:T(8,128)(2,1)}, u32[]{:S(2)}) copy-start(bf16[16,2,128,256]{3,2,1,0:T(8,128)(2,1)} %basis.1) | copy-start | bytes 6291460
  26.2 8.5 %copy-start.1 = (bf16[16,2,128,128]{3,2,1,0:T(8,128)(2,1)S(1)}, bf16[16,2,128,128]{3,2,1,0:T(8,128)(2,1)}, u32[]{:S(2)}) copy-start(bf16[16,2,128,128]{3,2,1,0:T(8,128)(2,1)} %transfer.1) | copy-start | bytes 3145732
  26.2 3.3 %collective-permute-start.3 = (bf16[128,256]{1,0:T(8,128)(2,1)S(1)}, bf16[128,256]{1,0:T(8,128)(2,1)S(1)}, u32[]{:S(2)}, u32[]{:S(2)}) collective-permute-start(bf16[128,256]{1,0:T(8,128)(2,1)S(1)} %get-tuple-element.18), channel_id=1, source_target_pairs={{0,1},{1,0},{2,3},{3,2},{4,5},{5,4},{6,7},{7,6},{8,9},{9,8},{10,11... | collective-permute-start | bytes 196616 | tf_op jit(solution)/shard_map/ppermute | solution.py:247
  29.5 0.6 %copy-start.3 = (f32[64,128]{1,0:T(8,128)}, f32[64,128]{1,0:T(8,128)S(1)}, u32[]{:S(2)}) copy-start(f32[64,128]{1,0:T(8,128)S(1)} %shard_map.93.field) | copy-start | bytes 98308
  30.1 8.4 %collective-permute-start.4 = (bf16[64,256]{1,0:T(8,128)(2,1)S(1)}, bf16[64,256]{1,0:T(8,128)(2,1)S(1)}, u32[]{:S(2)}, u32[]{:S(2)}) collective-permute-start(bf16[64,256]{1,0:T(8,128)(2,1)S(1)} %get-tuple-element.20), channel_id=1, source_target_pairs={{0,2},{1,3},{2,0},{3,1},{4,6},{5,7},{6,4},{7,5},{8,10},{9,11},{10,... | collective-permute-start | bytes 98312 | tf_op jit(solution)/shard_map/ppermute | solution.py:247
  34.6 0.8 %copy-start.4 = (f32[64,128]{1,0:T(8,128)S(1)}, f32[64,128]{1,0:T(8,128)}, u32[]{:S(2)}) copy-start(f32[64,128]{1,0:T(8,128)} %copy-done.3) | copy-start | bytes 98308

commit v3 on v2

--- a/solution.py
+++ b/solution.py
@@ -46,7 +46,7 @@
 
 def up_kernel(
     leaves, top_dev, own, charges_hbm, basis_hbm, transfer_hbm, parents, coefs, message,
-    charges, basis, transfer, coef, rows, own_coef, own_parent, arrived,
+    charges, basis, transfer, held, coef, rows, own_coef, own_parent, arrived,
 ):
     rank = basis.shape[2]
     branch = leaves // top_dev
@@ -63,19 +63,24 @@
     coef_rows = leaves * own
     stream.wait(0)
     for leaf in range(leaves):
-        if leaf % branch == 0:
-            stream.wait(1 + leaf // branch)
         source = charges[leaf].reshape(count, charges.shape[3])
-        product = dot(source, basis[leaf].reshape(2 * rank, -1), ALONG_LAST)
-        coef[leaf] = complex_rows(product)
-        own_coef[own * leaf : own * (leaf + 1), :] = coef[leaf, pl.ds(first, own), :]
+        held[leaf] = source
         start = coef_rows + 2 * count * leaf
         message[start : start + count, :] = source[:, :rank]
         message[start + count : start + 2 * count, :] = source[:, rank:]
+    for leaf in range(leaves):
+        if leaf % (2 * branch) == 0:
+            stream.wait(1 + leaf // branch)
+            stream.wait(2 + leaf // branch)
+        product = dot(held[leaf], basis[leaf].reshape(2 * rank, -1), ALONG_LAST)
+        coef[leaf] = complex_rows(product)
+    for leaf in range(leaves):
+        own_coef[own * leaf : own * (leaf + 1), :] = coef[leaf, pl.ds(first, own), :]
     coefs[...] = own_coef[...].astype(BF16)
     message[:coef_rows, :] = own_coef[...].astype(BF16)
     for top in range(top_dev):
         stream.wait(1 + top_dev + top)
+    for top in range(top_dev):
         total = jnp.zeros((count, rank), F32)
         for leaf in range(top * branch, (top + 1) * branch):
             value = coef[leaf].astype(BF16).astype(F32)
@@ -88,7 +93,7 @@
 
 def near_kernel(
     leaves, own, near_hbm, places_hbm, message, even_side, odd_side, blocks_hbm, kept, sent, sources,
-    near_list, places, blocks, table, coef_table, coef_wide, listed, tabled, arrived,
+    near_list, places, blocks, table, held, coef_table, coef_wide, listed, tabled, arrived,
 ):
     points = blocks.shape[4]
     rank = message.shape[1]
@@ -120,14 +125,22 @@
         lists.wait(i)
     for i in range(6):
         tables.wait(i)
-    others = []
     for leaf in range(leaves):
         place = (near_list[0, leaf] - first_leaf + leaves) * each
         value = table[pl.ds(pl.multiple_of(place, each), each), :]
-        value = jnp.concatenate([value[:count], value[count:]], axis=1)
+        held[leaf] = jnp.concatenate([value[:count], value[count:]], axis=1)
+    coef_wide[...] = coef_table[...].astype(F32)
+    for leaf in range(leaves):
+        for slot in range(1, places.shape[0]):
+            place = pl.multiple_of((places[slot, leaf] - first_leaf + leaves) * own, own)
+            sources[own * leaf : own * (leaf + 1), rank * (slot - 1) : rank * slot] = coef_wide[
+                pl.ds(place, own), :
+            ]
+    others = []
+    for leaf in range(leaves):
         if leaf % step == 0:
             stream.wait(leaf // step)
-        product = dot(value, blocks[leaf, 0].reshape(2 * points, points), ALONG_LAST)
+        product = dot(held[leaf], blocks[leaf, 0].reshape(2 * points, points), ALONG_LAST)
         value = complex_rows(product)
         for part in range(2):
             row = 2 * own * leaf + own * part
@@ -136,13 +149,6 @@
             kept[row : row + own, :] = jnp.where(core == 0, first, second)
             others.append(jnp.where(core == 0, second, first))
     sent[...] = jnp.concatenate(others).astype(BF16)
-    coef_wide[...] = coef_table[...].astype(F32)
-    for leaf in range(leaves):
-        for slot in range(1, places.shape[0]):
-            place = pl.multiple_of((places[slot, leaf] - first_leaf + leaves) * own, own)
-            sources[own * leaf : own * (leaf + 1), rank * (slot - 1) : rank * slot] = coef_wide[
-                pl.ds(place, own), :
-            ]
 
 
 def coupling_kernel(leaves, own, distant, sources, coupling, field):
@@ -177,23 +183,23 @@
 
 
 def down_kernel(
-    leaves, own, tops_hbm, gathered, top_hbm, transfer, basis, field, result,
-    tops, top_coupling, table, listed, arrived,
+    leaves, own, tops_hbm, gathered, top_coupling, transfer, basis_hbm, field, result,
+    tops, basis, table, listed, arrived,
 ):
-    rank = basis.shape[2]
+    rank = transfer.shape[2]
     top_dev = top_coupling.shape[0]
     slots = top_coupling.shape[1]
     branch = leaves // top_dev
     lists = Stream([(tops_hbm, tops)], listed, 1)
-    stream = Stream([(top_hbm.at[top], top_coupling.at[top]) for top in range(top_dev)], arrived, 4)
+    stream = Stream([(basis_hbm, basis)], arrived, 1)
     table[...] = gathered[...].astype(F32).reshape(table.shape)
     lists.wait(0)
+    pairs = []
     for top in range(top_dev):
         values = []
         for slot in range(slots):
             values.append(table[pl.ds(pl.multiple_of(tops[top, slot] * own, own), own), :])
         value = jnp.concatenate(values, axis=1).astype(BF16)
-        stream.wait(top)
         weights = jnp.concatenate(
             [top_coupling[top, slot].reshape(2 * rank, rank) for slot in range(slots)], axis=1
         )
@@ -201,10 +207,12 @@
         for leaf in range(top * branch, (top + 1) * branch):
             down = complex_rows(dot(top_field, transfer[leaf].reshape(2 * rank, rank), ALONG_LAST))
             value = (down + field[own * leaf : own * (leaf + 1), :]).astype(BF16).astype(F32)
-            pair = jnp.concatenate([value, turned(value)], axis=1).astype(BF16)
-            result[own * leaf : own * (leaf + 1), :] = dot(
-                pair, basis[leaf].reshape(2 * rank, -1), ALONG_ROWS
-            )
+            pairs.append(jnp.concatenate([value, turned(value)], axis=1).astype(BF16))
+    stream.wait(0)
+    for leaf in range(leaves):
+        result[own * leaf : own * (leaf + 1), :] = dot(
+            pairs[leaf], basis[leaf].reshape(2 * rank, -1), ALONG_ROWS
+        )
 
 
 VMEM = pl.BlockSpec(memory_space=pltpu.VMEM)
@@ -276,6 +284,7 @@
             pltpu.VMEM(charges.shape, BF16),
             pltpu.VMEM(basis.shape, BF16),
             pltpu.VMEM(transfer.shape, BF16),
+            pltpu.VMEM((leaves, count, points), BF16),
             pltpu.VMEM((leaves, count, rank), F32),
             pltpu.VMEM((count, rank), F32),
             pltpu.VMEM((coef_rows, rank), F32),
@@ -303,6 +312,7 @@
             pltpu.SMEM((coupling_list.shape[1], leaves), jnp.int32),
             pltpu.VMEM(near_blocks.shape, BF16),
             pltpu.VMEM((3 * leaves * 2 * count, rank), BF16),
+            pltpu.VMEM((leaves, count, points), BF16),
             pltpu.VMEM((3 * coef_rows, rank), BF16),
             pltpu.VMEM((3 * coef_rows, rank), F32),
             pltpu.SemaphoreType.DMA((2,)),
@@ -315,6 +325,17 @@
         8,
     )
     received = flipped(sent, "rhs", 1)
+    mine, sent = call(
+        functools.partial(half_kernel, leaves, own),
+        [((leaves * own, points), F32), ((leaves * own, points), BF16)],
+        [],
+        (kept, received),
+        {},
+        2 * 10**9,
+        2,
+    )
+    sources, mine = lax.optimization_barrier((sources, mine))
+    received = flipped(sent, "rhs", 2)
     (field,) = call(
         functools.partial(coupling_kernel, leaves, own),
         [((coef_rows, rank), F32)],
@@ -324,28 +345,18 @@
         2 * 10**9,
         6,
     )
-    mine, sent = call(
-        functools.partial(half_kernel, leaves, own),
-        [((leaves * own, points), F32), ((leaves * own, points), BF16)],
-        [],
-        (kept, received),
-        {},
-        10**7,
-        2,
-    )
-    received = flipped(sent, "rhs", 2)
     (far_part,) = call(
         functools.partial(down_kernel, leaves, own),
         [((leaves * own, points), F32)],
         [
             pltpu.SMEM(top_list.shape, jnp.int32),
-            pltpu.VMEM(top_coupling.shape, BF16),
+            pltpu.VMEM(basis.shape, BF16),
             pltpu.VMEM((groups * parent_rows, rank), F32),
             pltpu.SemaphoreType.DMA((1,)),
-            pltpu.SemaphoreType.DMA((top_dev,)),
+            pltpu.SemaphoreType.DMA((1,)),
         ],
         (top_list, gathered, top_coupling, transfer, basis, field),
-        {0: HBM, 2: HBM},
+        {0: HBM, 4: HBM},
         2 * 10**9,
         6,
     )

time: 39.5 us -> 35.6 us (0.901)
  the two profiles are of different devices: /device:TPU:2 before, /device:TPU:1 now
where the time goes in v3:
time: 35.6 us; the launch traced here: 35.4 us
  starting transfers between devices  24.6 us (69%)
  Pallas kernels  10.7 us (30%)
    all_to_all x1, starting transfers between devices, local(): gathered = lax.all_to_all(parents, 'leaf', 0, 0, tiled=True)  11.1 us
    pallas_call x6, Pallas kernels, call(): pl.pallas_call(kernel, out_shape=[jax.ShapeDtypeStruct(*shape) for shape...  10.7 us
    ppermute x2, starting transfers between devices, flipped(): return lax.ppermute(value, axis, [(i, i ^ bit) for i in range(count)])  5.9 us
    ppermute x2, starting transfers between devices, paired(): return lax.ppermute(value, axis, pairs)  5.25 us
    ppermute x1, starting transfers between devices, shifted(): lax.ppermute(value, axis, [(i, (i - step) % count) for i in range(count)])  2.31 us
  transfers between devices with their start and end apart: 6, of which 0 were waited for; matrix products, arithmetic and copies ran while one was open for 0% of the time, Pallas kernels for 19%

profile of v3, /device:TPU:1, one launch (start us, length us, event | category | flops | bytes accessed | tf_op | source)
XLA Modules:
  0.0 35.4 jit_solution(1514637072526374528)
XLA Ops:
  0.0 3.1 %shard_map.91 = (bf16[64,16,128]{2,1,0:T(8,128)(2,1)}, bf16[64,128]{1,0:T(8,128)(2,1)S(1)}, bf16[576,128]{1,0:T(8,128)(2,1)S(1)}) custom-call(bf16[16,8,2,256]{3,2,1,0:T(2,128)(2,1)} %charges_hbm.1, bf16[16,2,128,256]{3,2,1,0:T(8,128)(2,1)} %basis_hbm.3, bf16[16,2,128,128]{3,2,1,0:T(8,128)(2,1)} %transfer.1), custom_call_target="tpu_custom_call" | custom-call | flops 200000000 | bytes 4194304 | tf_op jit(solution)/shard_map/pallas_call | solution.py:229
  3.2 0.7 %collective-permute-start.2 = (bf16[576,128]{1,0:T(8,128)(2,1)S(1)}, bf16[576,128]{1,0:T(8,128)(2,1)S(1)}, u32[]{:S(2)}, u32[]{:S(2)}) collective-permute-start(bf16[576,128]{1,0:T(8,128)(2,1)S(1)} %get-tuple-element.17.message), channel_id=1, source_target_pairs={{4,8},{8,4},{12,16},{16,12},{20,24},{24,20},{28,32},{32,28},{36,40... | collective-permute-start | bytes 442376 | tf_op jit(solution)/shard_map/ppermute | solution.py:250
  3.8 4.6 %collective-permute-start.1 = (bf16[576,128]{1,0:T(8,128)(2,1)S(1)}, bf16[576,128]{1,0:T(8,128)(2,1)S(1)}, u32[]{:S(2)}, u32[]{:S(2)}) collective-permute-start(bf16[576,128]{1,0:T(8,128)(2,1)S(1)} %get-tuple-element.17.message), channel_id=1, source_target_pairs={{0,4},{4,0},{8,12},{12,8},{16,20},{20,16},{24,28},{28,24},{32,36},... | collective-permute-start | bytes 442376 | tf_op jit(solution)/shard_map/ppermute | solution.py:250
  8.4 11.1 %all-to-all-start = ((bf16[64,16,128]{2,1,0:T(8,128)(2,1)}), bf16[64,16,128]{2,1,0:T(8,128)(2,1)S(1)}, u32[]{:S(2)}, u32[]{:S(2)}) async-start(bf16[64,16,128]{2,1,0:T(8,128)(2,1)} %get-tuple-element.15), calls=%async_computation | async-start | bytes 524288 | tf_op jit(solution)/shard_map/all_to_all | solution.py:299
  19.6 0.0 collective-permute-done.2.odd_side
  19.6 0.0 collective-permute-done.1.even_side
  19.6 3.5 %shard_map.92 = (f32[128,256]{1,0:T(8,128)S(1)}, bf16[128,256]{1,0:T(8,128)(2,1)S(1)}, f32[64,384]{1,0:T(8,128)S(1)}) custom-call(s32[1,16]{1,0:T(1,128)} %bitcast.3, s32[4,16]{1,0:T(4,128)} %bitcast.2, bf16[576,128]{1,0:T(8,128)(2,1)S(1)} %get-tuple-element.17.message, bf16[576,128]{1,0:T(8,128)(2,1)S(1)} %collective-permute-done.1.even_side, ...), custom_call_target="tpu_custom_call" | custom-call | flops 2000000000 | bytes 4194304 | tf_op jit(solution)/shard_map/pallas_call | solution.py:229
  23.1 0.0 copy-start.1
  23.1 1.6 %collective-permute-start.3 = (bf16[128,256]{1,0:T(8,128)(2,1)S(1)}, bf16[128,256]{1,0:T(8,128)(2,1)S(1)}, u32[]{:S(2)}, u32[]{:S(2)}) collective-permute-start(bf16[128,256]{1,0:T(8,128)(2,1)S(1)} %get-tuple-element.20), channel_id=1, source_target_pairs={{0,1},{1,0},{2,3},{3,2},{4,5},{5,4},{6,7},{7,6},{8,9},{9,8},{10,11... | collective-permute-start | bytes 196616 | tf_op jit(solution)/shard_map/ppermute | solution.py:255
  24.7 2.3 %collective-permute-start = (bf16[64,128]{1,0:T(8,128)(2,1)S(1)}, bf16[64,128]{1,0:T(8,128)(2,1)S(1)}, u32[]{:S(2)}, u32[]{:S(2)}) collective-permute-start(bf16[64,128]{1,0:T(8,128)(2,1)S(1)} %get-tuple-element.16), channel_id=1, source_target_pairs={{0,128},{4,132},{8,136},{12,140},{16,144},{20,148},{24,152},{28,15... | collective-permute-start | bytes 49160 | tf_op jit(solution)/shard_map/ppermute | solution.py:242
  27.0 0.0 collective-permute-done.3.received
  27.1 0.0 copy-start
  27.1 0.0 copy-start.2
  27.1 4.3 %collective-permute-start.4 = (bf16[64,256]{1,0:T(8,128)(2,1)S(1)}, bf16[64,256]{1,0:T(8,128)(2,1)S(1)}, u32[]{:S(2)}, u32[]{:S(2)}) collective-permute-start(bf16[64,256]{1,0:T(8,128)(2,1)S(1)} %get-tuple-element.24), channel_id=1, source_target_pairs={{0,2},{1,3},{2,0},{3,1},{4,6},{5,7},{6,4},{7,5},{8,10},{9,11},{10,... | collective-permute-start | bytes 98312 | tf_op jit(solution)/shard_map/ppermute | solution.py:255
  31.4 0.0 collective-permute-done.distant
  31.4 0.0 copy-done.1
  31.4 1.2 %shard_map.94.field = f32[64,128]{1,0:T(8,128)S(1)} custom-call(bf16[64,128]{1,0:T(8,128)(2,1)S(1)} %collective-permute-done.distant, f32[64,384]{1,0:T(8,128)S(1)} %get-tuple-element.22.sources, bf16[16,4,2,128,128]{4,3,2,1,0:T(8,128)(2,1)S(1)} %copy-done.1), custom_call_target="tpu_custom_call" | custom-call | flops 2000000000 | bytes 4194304 | tf_op jit(solution)/shard_map/pallas_call | solution.py:229
  32.6 0.0 all-to-all-done.gathered
  32.6 0.0 copy-done
  32.6 0.0 copy-done.2
  32.6 2.1 %shard_map.95.far = f32[64,256]{1,0:T(8,128)S(1)} custom-call(s32[4,4]{1,0:T(4,128)} %tops_hbm.1, bf16[64,16,128]{2,1,0:T(8,128)(2,1)S(1)} %all-to-all-done.gathered, bf16[4,4,2,128,128]{4,3,2,1,0:T(8,128)(2,1)S(1)} %copy-done.2, bf16[16,2,128,128]{3,2,1,0:T(8,128)(2,1)S(1)} %copy-done, bf16[16,2,128,256]{3,2,1,0:T(8,128)(2,1)} %basis_hbm.3, ...), custom_call_target="tpu_custom_call" | custom-call | flops 2000000000 | bytes 4194304 | tf_op jit(solution)/shard_map/pallas_call | solution.py:229
  34.8 0.0 collective-permute-done.4.received
  34.8 0.6 %shard_map.96 = bf16[16,2,2,256]{3,2,1,0:T(2,128)(2,1)} custom-call(f32[64,256]{1,0:T(8,128)S(1)} %shard_map.95.far, f32[64,256]{1,0:T(8,128)S(1)} %get-tuple-element.23.mine, bf16[64,256]{1,0:T(8,128)(2,1)S(1)} %collective-permute-done.4.received), custom_call_target="tpu_custom_call" | custom-call | flops 10000000 | bytes 4194304 | tf_op jit(solution)/shard_map/pallas_call | solution.py:229
  (1 shorter events, 0.0 us)
Async XLA Ops:
  3.2 16.4 %collective-permute-start.2 = (bf16[576,128]{1,0:T(8,128)(2,1)S(1)}, bf16[576,128]{1,0:T(8,128)(2,1)S(1)}, u32[]{:S(2)}, u32[]{:S(2)}) collective-permute-start(bf16[576,128]{1,0:T(8,128)(2,1)S(1)} %get-tuple-element.17.message), channel_id=1, source_target_pairs={{4,8},{8,4},{12,16},{16,12},{20,24},{24,20},{28,32},{32,28},{36,40... | collective-permute-start | bytes 442376 | tf_op jit(solution)/shard_map/ppermute | solution.py:250
  3.8 15.7 %collective-permute-start.1 = (bf16[576,128]{1,0:T(8,128)(2,1)S(1)}, bf16[576,128]{1,0:T(8,128)(2,1)S(1)}, u32[]{:S(2)}, u32[]{:S(2)}) collective-permute-start(bf16[576,128]{1,0:T(8,128)(2,1)S(1)} %get-tuple-element.17.message), channel_id=1, source_target_pairs={{0,4},{4,0},{8,12},{12,8},{16,20},{20,16},{24,28},{28,24},{32,36},... | collective-permute-start | bytes 442376 | tf_op jit(solution)/shard_map/ppermute | solution.py:250
  8.4 24.2 %all-to-all-start = ((bf16[64,16,128]{2,1,0:T(8,128)(2,1)}), bf16[64,16,128]{2,1,0:T(8,128)(2,1)S(1)}, u32[]{:S(2)}, u32[]{:S(2)}) async-start(bf16[64,16,128]{2,1,0:T(8,128)(2,1)} %get-tuple-element.15), calls=%async_computation | async-start | bytes 524288 | tf_op jit(solution)/shard_map/all_to_all | solution.py:299
  23.1 8.3 %copy-start.1 = (bf16[16,4,2,128,128]{4,3,2,1,0:T(8,128)(2,1)S(1)}, bf16[16,4,2,128,128]{4,3,2,1,0:T(8,128)(2,1)}, u32[]{:S(2)}) copy-start(bf16[16,4,2,128,128]{4,3,2,1,0:T(8,128)(2,1)} %coupling.1) | copy-start | bytes 12582916
  23.1 3.9 %collective-permute-start.3 = (bf16[128,256]{1,0:T(8,128)(2,1)S(1)}, bf16[128,256]{1,0:T(8,128)(2,1)S(1)}, u32[]{:S(2)}, u32[]{:S(2)}) collective-permute-start(bf16[128,256]{1,0:T(8,128)(2,1)S(1)} %get-tuple-element.20), channel_id=1, source_target_pairs={{0,1},{1,0},{2,3},{3,2},{4,5},{5,4},{6,7},{7,6},{8,9},{9,8},{10,11... | collective-permute-start | bytes 196616 | tf_op jit(solution)/shard_map/ppermute | solution.py:255
  24.7 6.7 %collective-permute-start = (bf16[64,128]{1,0:T(8,128)(2,1)S(1)}, bf16[64,128]{1,0:T(8,128)(2,1)S(1)}, u32[]{:S(2)}, u32[]{:S(2)}) collective-permute-start(bf16[64,128]{1,0:T(8,128)(2,1)S(1)} %get-tuple-element.16), channel_id=1, source_target_pairs={{0,128},{4,132},{8,136},{12,140},{16,144},{20,148},{24,152},{28,15... | collective-permute-start | bytes 49160 | tf_op jit(solution)/shard_map/ppermute | solution.py:242
  27.1 5.6 %copy-start = (bf16[16,2,128,128]{3,2,1,0:T(8,128)(2,1)S(1)}, bf16[16,2,128,128]{3,2,1,0:T(8,128)(2,1)}, u32[]{:S(2)}) copy-start(bf16[16,2,128,128]{3,2,1,0:T(8,128)(2,1)} %transfer.1) | copy-start | bytes 3145732
  27.1 5.5 %copy-start.2 = (bf16[4,4,2,128,128]{4,3,2,1,0:T(8,128)(2,1)S(1)}, bf16[4,4,2,128,128]{4,3,2,1,0:T(8,128)(2,1)}, u32[]{:S(2)}) copy-start(bf16[4,4,2,128,128]{4,3,2,1,0:T(8,128)(2,1)} %top_coupling.1) | copy-start | bytes 3145732
  27.1 7.7 %collective-permute-start.4 = (bf16[64,256]{1,0:T(8,128)(2,1)S(1)}, bf16[64,256]{1,0:T(8,128)(2,1)S(1)}, u32[]{:S(2)}, u32[]{:S(2)}) collective-permute-start(bf16[64,256]{1,0:T(8,128)(2,1)S(1)} %get-tuple-element.24), channel_id=1, source_target_pairs={{0,2},{1,3},{2,0},{3,1},{4,6},{5,7},{6,4},{7,5},{8,10},{9,11},{10,... | collective-permute-start | bytes 98312 | tf_op jit(solution)/shard_map/ppermute | solution.py:255

commit v4 on v3

--- a/solution.py
+++ b/solution.py
@@ -45,7 +45,7 @@
 
 
 def up_kernel(
-    leaves, top_dev, own, charges_hbm, basis_hbm, transfer_hbm, parents, coefs, message,
+    leaves, top_dev, own, charges_hbm, basis_hbm, transfer_hbm, blocks_hbm, parents, coefs, message, early,
     charges, basis, transfer, held, coef, rows, own_coef, own_parent, arrived,
 ):
     rank = basis.shape[2]
@@ -54,9 +54,10 @@
     stream = Stream(
         [(charges_hbm, charges)]
         + [(basis_hbm.at[part], basis.at[part]) for part in parts]
-        + [(transfer_hbm.at[part], transfer.at[part]) for part in parts],
+        + [(transfer_hbm.at[part], transfer.at[part]) for part in parts]
+        + [(blocks_hbm.at[pl.ds(0, early.shape[0])], early)],
         arrived,
-        1 + 2 * top_dev,
+        2 + 2 * top_dev,
     )
     count = charges.shape[1] * 2
     first = pl.multiple_of(lax.axis_index("rhs") * own, own)
@@ -88,11 +89,12 @@
             total += dot(pair, transfer[leaf].reshape(2 * rank, -1), ALONG_ROWS)
         rows[...] = total
         own_parent[own * top : own * (top + 1), :] = rows[pl.ds(first, own), :]
+    stream.wait(1 + 2 * top_dev)
     parents[...] = jnp.broadcast_to(own_parent[...].astype(BF16)[None], parents.shape)
 
 
 def near_kernel(
-    leaves, own, near_hbm, places_hbm, message, even_side, odd_side, blocks_hbm, kept, sent, sources,
+    leaves, own, near_hbm, places_hbm, message, even_side, odd_side, early, blocks_hbm, kept, sent, sources,
     near_list, places, blocks, table, held, coef_table, coef_wide, listed, tabled, arrived,
 ):
     points = blocks.shape[4]
@@ -117,8 +119,15 @@
         6,
     )
     step = 4
-    chunks = [pl.ds(leaf, step) for leaf in range(0, leaves, step)]
-    stream = Stream([(blocks_hbm.at[part], blocks.at[part]) for part in chunks], arrived, 4)
+    begin = early.shape[0]
+    stream = Stream(
+        [
+            (blocks_hbm.at[pl.ds(leaf, step)], blocks.at[pl.ds(leaf - begin, step)])
+            for leaf in range(begin, leaves, step)
+        ],
+        arrived,
+        4,
+    )
     first_leaf = me * leaves
     core = lax.axis_index("rhs") % 2
     for i in range(2):
@@ -138,9 +147,10 @@
             ]
     others = []
     for leaf in range(leaves):
-        if leaf % step == 0:
-            stream.wait(leaf // step)
-        product = dot(held[leaf], blocks[leaf, 0].reshape(2 * points, points), ALONG_LAST)
+        if leaf >= begin and leaf % step == 0:
+            stream.wait((leaf - begin) // step)
+        block = early[leaf, 0] if leaf < begin else blocks[leaf - begin, 0]
+        product = dot(held[leaf], block.reshape(2 * points, points), ALONG_LAST)
         value = complex_rows(product)
         for part in range(2):
             row = 2 * own * leaf + own * part
@@ -273,12 +283,13 @@
     groups = lax.axis_size("leaf")
     count, own = 2 * rhs_all, 2 * rhs_dev
     parent_rows, coef_rows = top_dev * own, leaves * own
-    parents, coefs, message = call(
+    parents, coefs, message, early = call(
         functools.partial(up_kernel, leaves, top_dev, own),
         [
             ((groups, parent_rows, rank), BF16),
             ((coef_rows, rank), BF16),
             ((coef_rows + leaves * 2 * count, rank), BF16),
+            ((leaves // 2, *near_blocks.shape[1:]), BF16),
         ],
         [
             pltpu.VMEM(charges.shape, BF16),
@@ -289,12 +300,12 @@
             pltpu.VMEM((count, rank), F32),
             pltpu.VMEM((coef_rows, rank), F32),
             pltpu.VMEM((parent_rows, rank), F32),
-            pltpu.SemaphoreType.DMA((1 + 2 * top_dev,)),
-        ],
-        (charges, basis, transfer),
-        {0: HBM, 1: HBM, 2: HBM},
+            pltpu.SemaphoreType.DMA((2 + 2 * top_dev,)),
+        ],
+        (charges, basis, transfer, near_blocks),
+        {0: HBM, 1: HBM, 2: HBM, 3: HBM},
         2 * 10**8,
-        8,
+        12,
     )
     gathered = lax.all_to_all(parents, "leaf", 0, 0, tiled=True)
     odd_side = paired(message, "leaf", 1)
@@ -310,17 +321,17 @@
         [
             pltpu.SMEM((1, leaves), jnp.int32),
             pltpu.SMEM((coupling_list.shape[1], leaves), jnp.int32),
-            pltpu.VMEM(near_blocks.shape, BF16),
+            pltpu.VMEM((leaves // 2, *near_blocks.shape[1:]), BF16),
             pltpu.VMEM((3 * leaves * 2 * count, rank), BF16),
             pltpu.VMEM((leaves, count, points), BF16),
             pltpu.VMEM((3 * coef_rows, rank), BF16),
             pltpu.VMEM((3 * coef_rows, rank), F32),
             pltpu.SemaphoreType.DMA((2,)),
             pltpu.SemaphoreType.DMA((6,)),
-            pltpu.SemaphoreType.DMA((leaves // 4,)),
-        ],
-        (near_list.T, coupling_list.T, message, even_side, odd_side, near_blocks),
-        {0: HBM, 1: HBM, 2: ANY, 3: ANY, 4: ANY, 5: HBM},
+            pltpu.SemaphoreType.DMA((leaves // 8,)),
+        ],
+        (near_list.T, coupling_list.T, message, even_side, odd_side, early, near_blocks),
+        {0: HBM, 1: HBM, 2: ANY, 3: ANY, 4: ANY, 6: HBM},
         2 * 10**9,
         8,
     )

time: 35.6 us -> 35.1 us (0.986)
  Pallas kernels: 10.7 us -> 10.1 us
    pallas_call x6, Pallas kernels: 10.7 us -> 10.1 us  [call(): pl.pallas_call(kernel, out_shape=[jax.ShapeDtypeStruct(*shape) for shape...]
  transfers between devices with their start and end apart: 6 -> 6, of which waited for: 0 -> 0; matrix products, arithmetic and copies ran while one was open for 0% -> 0% of each run, Pallas kernels for 19% -> 17%
where the time goes in v4:
time: 35.1 us; the launch traced here: 34.9 us
  starting transfers between devices  24.6 us (70%)
  Pallas kernels  10.1 us (29%)
    all_to_all x1, starting transfers between devices, local(): gathered = lax.all_to_all(parents, 'leaf', 0, 0, tiled=True)  11.1 us
    pallas_call x6, Pallas kernels, call(): pl.pallas_call(kernel, out_shape=[jax.ShapeDtypeStruct(*shape) for shape...  10.1 us
    ppermute x2, starting transfers between devices, flipped(): return lax.ppermute(value, axis, [(i, i ^ bit) for i in range(count)])  5.9 us
    ppermute x2, starting transfers between devices, paired(): return lax.ppermute(value, axis, pairs)  5.25 us
    ppermute x1, starting transfers between devices, shifted(): lax.ppermute(value, axis, [(i, (i - step) % count) for i in range(count)])  2.31 us
  transfers between devices with their start and end apart: 6, of which 0 were waited for; matrix products, arithmetic and copies ran while one was open for 0% of the time, Pallas kernels for 17%

profile of v4, /device:TPU:1, one launch (start us, length us, event | category | flops | bytes accessed | tf_op | source)
XLA Modules:
  0.0 34.9 jit_solution(14112970319015088931)
XLA Ops:
  0.0 3.4 %shard_map.91 = (bf16[64,16,128]{2,1,0:T(8,128)(2,1)}, bf16[64,128]{1,0:T(8,128)(2,1)S(1)}, bf16[576,128]{1,0:T(8,128)(2,1)S(1)}, bf16[8,1,2,256,256]{4,3,2,1,0:T(8,128)(2,1)S(1)}) custom-call(bf16[16,8,2,256]{3,2,1,0:T(2,128)(2,1)} %charges_hbm.1, bf16[16,2,128,256]{3,2,1,0:T(8,128)(2,1)} %basis_hbm.3, bf16[16,2,128,128]{3,2,1,0:T(8,128)(2,1)} %transfer.1, ...), custom_call_target="tpu_custom_call" | custom-call | flops 200000000 | bytes 4194304 | tf_op jit(solution)/shard_map/pallas_call | solution.py:239
  3.4 0.7 %collective-permute-start.2 = (bf16[576,128]{1,0:T(8,128)(2,1)S(1)}, bf16[576,128]{1,0:T(8,128)(2,1)S(1)}, u32[]{:S(2)}, u32[]{:S(2)}) collective-permute-start(bf16[576,128]{1,0:T(8,128)(2,1)S(1)} %get-tuple-element.18.message), channel_id=1, source_target_pairs={{4,8},{8,4},{12,16},{16,12},{20,24},{24,20},{28,32},{32,28},{36,40... | collective-permute-start | bytes 442376 | tf_op jit(solution)/shard_map/ppermute | solution.py:260
  4.1 4.6 %collective-permute-start.1 = (bf16[576,128]{1,0:T(8,128)(2,1)S(1)}, bf16[576,128]{1,0:T(8,128)(2,1)S(1)}, u32[]{:S(2)}, u32[]{:S(2)}) collective-permute-start(bf16[576,128]{1,0:T(8,128)(2,1)S(1)} %get-tuple-element.18.message), channel_id=1, source_target_pairs={{0,4},{4,0},{8,12},{12,8},{16,20},{20,16},{24,28},{28,24},{32,36},... | collective-permute-start | bytes 442376 | tf_op jit(solution)/shard_map/ppermute | solution.py:260
  8.7 11.1 %all-to-all-start = ((bf16[64,16,128]{2,1,0:T(8,128)(2,1)}), bf16[64,16,128]{2,1,0:T(8,128)(2,1)S(1)}, u32[]{:S(2)}, u32[]{:S(2)}) async-start(bf16[64,16,128]{2,1,0:T(8,128)(2,1)} %get-tuple-element.16), calls=%async_computation | async-start | bytes 524288 | tf_op jit(solution)/shard_map/all_to_all | solution.py:310
  19.8 0.0 collective-permute-done.2.odd_side
  19.8 0.0 collective-permute-done.1.even_side
  19.9 2.7 %shard_map.92 = (f32[128,256]{1,0:T(8,128)S(1)}, bf16[128,256]{1,0:T(8,128)(2,1)S(1)}, f32[64,384]{1,0:T(8,128)S(1)}) custom-call(s32[1,16]{1,0:T(1,128)} %bitcast.3, s32[4,16]{1,0:T(4,128)} %bitcast.2, bf16[576,128]{1,0:T(8,128)(2,1)S(1)} %get-tuple-element.18.message, bf16[576,128]{1,0:T(8,128)(2,1)S(1)} %collective-permute-done.1.even_side, ...), custom_call_target="tpu_custom_call" | custom-call | flops 2000000000 | bytes 4194304 | tf_op jit(solution)/shard_map/pallas_call | solution.py:239
  22.6 0.0 copy-start.1
  22.6 1.6 %collective-permute-start.3 = (bf16[128,256]{1,0:T(8,128)(2,1)S(1)}, bf16[128,256]{1,0:T(8,128)(2,1)S(1)}, u32[]{:S(2)}, u32[]{:S(2)}) collective-permute-start(bf16[128,256]{1,0:T(8,128)(2,1)S(1)} %get-tuple-element.22), channel_id=1, source_target_pairs={{0,1},{1,0},{2,3},{3,2},{4,5},{5,4},{6,7},{7,6},{8,9},{9,8},{10,11... | collective-permute-start | bytes 196616 | tf_op jit(solution)/shard_map/ppermute | solution.py:265
  24.2 2.3 %collective-permute-start = (bf16[64,128]{1,0:T(8,128)(2,1)S(1)}, bf16[64,128]{1,0:T(8,128)(2,1)S(1)}, u32[]{:S(2)}, u32[]{:S(2)}) collective-permute-start(bf16[64,128]{1,0:T(8,128)(2,1)S(1)} %get-tuple-element.17), channel_id=1, source_target_pairs={{0,128},{4,132},{8,136},{12,140},{16,144},{20,148},{24,152},{28,15... | collective-permute-start | bytes 49160 | tf_op jit(solution)/shard_map/ppermute | solution.py:252
  26.5 0.0 collective-permute-done.3.received
  26.5 0.0 copy-start
  26.5 0.0 copy-start.2
  26.5 4.3 %collective-permute-start.4 = (bf16[64,256]{1,0:T(8,128)(2,1)S(1)}, bf16[64,256]{1,0:T(8,128)(2,1)S(1)}, u32[]{:S(2)}, u32[]{:S(2)}) collective-permute-start(bf16[64,256]{1,0:T(8,128)(2,1)S(1)} %get-tuple-element.26), channel_id=1, source_target_pairs={{0,2},{1,3},{2,0},{3,1},{4,6},{5,7},{6,4},{7,5},{8,10},{9,11},{10,... | collective-permute-start | bytes 98312 | tf_op jit(solution)/shard_map/ppermute | solution.py:265
  30.8 0.0 collective-permute-done.distant
  30.8 0.0 copy-done.1
  30.9 1.2 %shard_map.94.field = f32[64,128]{1,0:T(8,128)S(1)} custom-call(bf16[64,128]{1,0:T(8,128)(2,1)S(1)} %collective-permute-done.distant, f32[64,384]{1,0:T(8,128)S(1)} %get-tuple-element.24.sources, bf16[16,4,2,128,128]{4,3,2,1,0:T(8,128)(2,1)S(1)} %copy-done.1), custom_call_target="tpu_custom_call" | custom-call | flops 2000000000 | bytes 4194304 | tf_op jit(solution)/shard_map/pallas_call | solution.py:239
  32.0 0.0 all-to-all-done.gathered
  32.1 0.0 copy-done
  32.1 0.0 copy-done.2
  32.1 2.1 %shard_map.95.far = f32[64,256]{1,0:T(8,128)S(1)} custom-call(s32[4,4]{1,0:T(4,128)} %tops_hbm.1, bf16[64,16,128]{2,1,0:T(8,128)(2,1)S(1)} %all-to-all-done.gathered, bf16[4,4,2,128,128]{4,3,2,1,0:T(8,128)(2,1)S(1)} %copy-done.2, bf16[16,2,128,128]{3,2,1,0:T(8,128)(2,1)S(1)} %copy-done, bf16[16,2,128,256]{3,2,1,0:T(8,128)(2,1)} %basis_hbm.3, ...), custom_call_target="tpu_custom_call" | custom-call | flops 2000000000 | bytes 4194304 | tf_op jit(solution)/shard_map/pallas_call | solution.py:239
  34.2 0.0 collective-permute-done.4.received
  34.2 0.6 %shard_map.96 = bf16[16,2,2,256]{3,2,1,0:T(2,128)(2,1)} custom-call(f32[64,256]{1,0:T(8,128)S(1)} %shard_map.95.far, f32[64,256]{1,0:T(8,128)S(1)} %get-tuple-element.25.mine, bf16[64,256]{1,0:T(8,128)(2,1)S(1)} %collective-permute-done.4.received), custom_call_target="tpu_custom_call" | custom-call | flops 10000000 | bytes 4194304 | tf_op jit(solution)/shard_map/pallas_call | solution.py:239
  (1 shorter events, 0.0 us)
Async XLA Ops:
  3.4 16.4 %collective-permute-start.2 = (bf16[576,128]{1,0:T(8,128)(2,1)S(1)}, bf16[576,128]{1,0:T(8,128)(2,1)S(1)}, u32[]{:S(2)}, u32[]{:S(2)}) collective-permute-start(bf16[576,128]{1,0:T(8,128)(2,1)S(1)} %get-tuple-element.18.message), channel_id=1, source_target_pairs={{4,8},{8,4},{12,16},{16,12},{20,24},{24,20},{28,32},{32,28},{36,40... | collective-permute-start | bytes 442376 | tf_op jit(solution)/shard_map/ppermute | solution.py:260
  4.1 15.7 %collective-permute-start.1 = (bf16[576,128]{1,0:T(8,128)(2,1)S(1)}, bf16[576,128]{1,0:T(8,128)(2,1)S(1)}, u32[]{:S(2)}, u32[]{:S(2)}) collective-permute-start(bf16[576,128]{1,0:T(8,128)(2,1)S(1)} %get-tuple-element.18.message), channel_id=1, source_target_pairs={{0,4},{4,0},{8,12},{12,8},{16,20},{20,16},{24,28},{28,24},{32,36},... | collective-permute-start | bytes 442376 | tf_op jit(solution)/shard_map/ppermute | solution.py:260
  8.7 23.4 %all-to-all-start = ((bf16[64,16,128]{2,1,0:T(8,128)(2,1)}), bf16[64,16,128]{2,1,0:T(8,128)(2,1)S(1)}, u32[]{:S(2)}, u32[]{:S(2)}) async-start(bf16[64,16,128]{2,1,0:T(8,128)(2,1)} %get-tuple-element.16), calls=%async_computation | async-start | bytes 524288 | tf_op jit(solution)/shard_map/all_to_all | solution.py:310
  22.6 8.3 %copy-start.1 = (bf16[16,4,2,128,128]{4,3,2,1,0:T(8,128)(2,1)S(1)}, bf16[16,4,2,128,128]{4,3,2,1,0:T(8,128)(2,1)}, u32[]{:S(2)}) copy-start(bf16[16,4,2,128,128]{4,3,2,1,0:T(8,128)(2,1)} %coupling.1) | copy-start | bytes 12582916
  22.6 3.9 %collective-permute-start.3 = (bf16[128,256]{1,0:T(8,128)(2,1)S(1)}, bf16[128,256]{1,0:T(8,128)(2,1)S(1)}, u32[]{:S(2)}, u32[]{:S(2)}) collective-permute-start(bf16[128,256]{1,0:T(8,128)(2,1)S(1)} %get-tuple-element.22), channel_id=1, source_target_pairs={{0,1},{1,0},{2,3},{3,2},{4,5},{5,4},{6,7},{7,6},{8,9},{9,8},{10,11... | collective-permute-start | bytes 196616 | tf_op jit(solution)/shard_map/ppermute | solution.py:265
  24.2 6.7 %collective-permute-start = (bf16[64,128]{1,0:T(8,128)(2,1)S(1)}, bf16[64,128]{1,0:T(8,128)(2,1)S(1)}, u32[]{:S(2)}, u32[]{:S(2)}) collective-permute-start(bf16[64,128]{1,0:T(8,128)(2,1)S(1)} %get-tuple-element.17), channel_id=1, source_target_pairs={{0,128},{4,132},{8,136},{12,140},{16,144},{20,148},{24,152},{28,15... | collective-permute-start | bytes 49160 | tf_op jit(solution)/shard_map/ppermute | solution.py:252
  26.5 5.5 %copy-start = (bf16[16,2,128,128]{3,2,1,0:T(8,128)(2,1)S(1)}, bf16[16,2,128,128]{3,2,1,0:T(8,128)(2,1)}, u32[]{:S(2)}) copy-start(bf16[16,2,128,128]{3,2,1,0:T(8,128)(2,1)} %transfer.1) | copy-start | bytes 3145732
  26.5 5.5 %copy-start.2 = (bf16[4,4,2,128,128]{4,3,2,1,0:T(8,128)(2,1)S(1)}, bf16[4,4,2,128,128]{4,3,2,1,0:T(8,128)(2,1)}, u32[]{:S(2)}) copy-start(bf16[4,4,2,128,128]{4,3,2,1,0:T(8,128)(2,1)} %top_coupling.1) | copy-start | bytes 3145732
  26.5 7.7 %collective-permute-start.4 = (bf16[64,256]{1,0:T(8,128)(2,1)S(1)}, bf16[64,256]{1,0:T(8,128)(2,1)S(1)}, u32[]{:S(2)}, u32[]{:S(2)}) collective-permute-start(bf16[64,256]{1,0:T(8,128)(2,1)S(1)} %get-tuple-element.26), channel_id=1, source_target_pairs={{0,2},{1,3},{2,0},{3,1},{4,6},{5,7},{6,4},{7,5},{8,10},{9,11},{10,... | collective-permute-start | bytes 98312 | tf_op jit(solution)/shard_map/ppermute | solution.py:265

commit v5 on v4

--- a/solution.py
+++ b/solution.py
@@ -104,6 +104,16 @@
     each = size // leaves
     count = each // 2
     lists = Stream([(near_hbm, near_list), (places_hbm, places)], listed, 2)
+    step = 4
+    begin = early.shape[0]
+    stream = Stream(
+        [
+            (blocks_hbm.at[pl.ds(leaf, step)], blocks.at[pl.ds(leaf - begin, step)])
+            for leaf in range(begin, leaves, step)
+        ],
+        arrived,
+        4,
+    )
     me = lax.axis_index("leaf")
     order = ((even_side, 2 - 2 * (me % 2)), (message, 1), (odd_side, 2 * (me % 2)))
     tables = Stream(
@@ -117,16 +127,6 @@
         ],
         tabled,
         6,
-    )
-    step = 4
-    begin = early.shape[0]
-    stream = Stream(
-        [
-            (blocks_hbm.at[pl.ds(leaf, step)], blocks.at[pl.ds(leaf - begin, step)])
-            for leaf in range(begin, leaves, step)
-        ],
-        arrived,
-        4,
     )
     first_leaf = me * leaves
     core = lax.axis_index("rhs") % 2

time: 35.1 us -> 34.8 us (level)
  no operation moved by 1% of the time
where the time goes in v5:
time: 34.8 us; the launch traced here: 34.6 us
  starting transfers between devices  24.6 us (71%)
  Pallas kernels  9.82 us (28%)
    all_to_all x1, starting transfers between devices, local(): gathered = lax.all_to_all(parents, 'leaf', 0, 0, tiled=True)  11.1 us
    pallas_call x6, Pallas kernels, call(): pl.pallas_call(kernel, out_shape=[jax.ShapeDtypeStruct(*shape) for shape...  9.82 us
    ppermute x2, starting transfers between devices, flipped(): return lax.ppermute(value, axis, [(i, i ^ bit) for i in range(count)])  5.9 us
    ppermute x2, starting transfers between devices, paired(): return lax.ppermute(value, axis, pairs)  5.25 us
    ppermute x1, starting transfers between devices, shifted(): lax.ppermute(value, axis, [(i, (i - step) % count) for i in range(count)])  2.31 us
  transfers between devices with their start and end apart: 6, of which 0 were waited for; matrix products, arithmetic and copies ran while one was open for 0% of the time, Pallas kernels for 17%

profile of v5, /device:TPU:1, one launch (start us, length us, event | category | flops | bytes accessed | tf_op | source)
XLA Modules:
  0.0 34.6 jit_solution(357625463584120309)
XLA Ops:
  0.0 3.4 %shard_map.91 = (bf16[64,16,128]{2,1,0:T(8,128)(2,1)}, bf16[64,128]{1,0:T(8,128)(2,1)S(1)}, bf16[576,128]{1,0:T(8,128)(2,1)S(1)}, bf16[8,1,2,256,256]{4,3,2,1,0:T(8,128)(2,1)S(1)}) custom-call(bf16[16,8,2,256]{3,2,1,0:T(2,128)(2,1)} %charges_hbm.1, bf16[16,2,128,256]{3,2,1,0:T(8,128)(2,1)} %basis_hbm.3, bf16[16,2,128,128]{3,2,1,0:T(8,128)(2,1)} %transfer.1, ...), custom_call_target="tpu_custom_call" | custom-call | flops 200000000 | bytes 4194304 | tf_op jit(solution)/shard_map/pallas_call | solution.py:239
  3.4 0.7 %collective-permute-start.2 = (bf16[576,128]{1,0:T(8,128)(2,1)S(1)}, bf16[576,128]{1,0:T(8,128)(2,1)S(1)}, u32[]{:S(2)}, u32[]{:S(2)}) collective-permute-start(bf16[576,128]{1,0:T(8,128)(2,1)S(1)} %get-tuple-element.18.message), channel_id=1, source_target_pairs={{4,8},{8,4},{12,16},{16,12},{20,24},{24,20},{28,32},{32,28},{36,40... | collective-permute-start | bytes 442376 | tf_op jit(solution)/shard_map/ppermute | solution.py:260
  4.1 4.6 %collective-permute-start.1 = (bf16[576,128]{1,0:T(8,128)(2,1)S(1)}, bf16[576,128]{1,0:T(8,128)(2,1)S(1)}, u32[]{:S(2)}, u32[]{:S(2)}) collective-permute-start(bf16[576,128]{1,0:T(8,128)(2,1)S(1)} %get-tuple-element.18.message), channel_id=1, source_target_pairs={{0,4},{4,0},{8,12},{12,8},{16,20},{20,16},{24,28},{28,24},{32,36},... | collective-permute-start | bytes 442376 | tf_op jit(solution)/shard_map/ppermute | solution.py:260
  8.7 11.1 %all-to-all-start = ((bf16[64,16,128]{2,1,0:T(8,128)(2,1)}), bf16[64,16,128]{2,1,0:T(8,128)(2,1)S(1)}, u32[]{:S(2)}, u32[]{:S(2)}) async-start(bf16[64,16,128]{2,1,0:T(8,128)(2,1)} %get-tuple-element.16), calls=%async_computation | async-start | bytes 524288 | tf_op jit(solution)/shard_map/all_to_all | solution.py:310
  19.8 0.0 collective-permute-done.2.odd_side
  19.8 0.0 collective-permute-done.1.even_side
  19.9 2.4 %shard_map.92 = (f32[128,256]{1,0:T(8,128)S(1)}, bf16[128,256]{1,0:T(8,128)(2,1)S(1)}, f32[64,384]{1,0:T(8,128)S(1)}) custom-call(s32[1,16]{1,0:T(1,128)} %bitcast.3, s32[4,16]{1,0:T(4,128)} %bitcast.2, bf16[576,128]{1,0:T(8,128)(2,1)S(1)} %get-tuple-element.18.message, bf16[576,128]{1,0:T(8,128)(2,1)S(1)} %collective-permute-done.1.even_side, ...), custom_call_target="tpu_custom_call" | custom-call | flops 2000000000 | bytes 4194304 | tf_op jit(solution)/shard_map/pallas_call | solution.py:239
  22.3 0.0 copy-start.1
  22.3 1.6 %collective-permute-start.3 = (bf16[128,256]{1,0:T(8,128)(2,1)S(1)}, bf16[128,256]{1,0:T(8,128)(2,1)S(1)}, u32[]{:S(2)}, u32[]{:S(2)}) collective-permute-start(bf16[128,256]{1,0:T(8,128)(2,1)S(1)} %get-tuple-element.22), channel_id=1, source_target_pairs={{0,1},{1,0},{2,3},{3,2},{4,5},{5,4},{6,7},{7,6},{8,9},{9,8},{10,11... | collective-permute-start | bytes 196616 | tf_op jit(solution)/shard_map/ppermute | solution.py:265
  23.9 2.3 %collective-permute-start = (bf16[64,128]{1,0:T(8,128)(2,1)S(1)}, bf16[64,128]{1,0:T(8,128)(2,1)S(1)}, u32[]{:S(2)}, u32[]{:S(2)}) collective-permute-start(bf16[64,128]{1,0:T(8,128)(2,1)S(1)} %get-tuple-element.17), channel_id=1, source_target_pairs={{0,128},{4,132},{8,136},{12,140},{16,144},{20,148},{24,152},{28,15... | collective-permute-start | bytes 49160 | tf_op jit(solution)/shard_map/ppermute | solution.py:252
  26.2 0.0 collective-permute-done.3.received
  26.2 0.0 copy-start
  26.2 0.0 copy-start.2
  26.2 4.3 %collective-permute-start.4 = (bf16[64,256]{1,0:T(8,128)(2,1)S(1)}, bf16[64,256]{1,0:T(8,128)(2,1)S(1)}, u32[]{:S(2)}, u32[]{:S(2)}) collective-permute-start(bf16[64,256]{1,0:T(8,128)(2,1)S(1)} %get-tuple-element.26), channel_id=1, source_target_pairs={{0,2},{1,3},{2,0},{3,1},{4,6},{5,7},{6,4},{7,5},{8,10},{9,11},{10,... | collective-permute-start | bytes 98312 | tf_op jit(solution)/shard_map/ppermute | solution.py:265
  30.5 0.0 collective-permute-done.distant
  30.5 0.0 copy-done.1
  30.5 1.2 %shard_map.94.field = f32[64,128]{1,0:T(8,128)S(1)} custom-call(bf16[64,128]{1,0:T(8,128)(2,1)S(1)} %collective-permute-done.distant, f32[64,384]{1,0:T(8,128)S(1)} %get-tuple-element.24.sources, bf16[16,4,2,128,128]{4,3,2,1,0:T(8,128)(2,1)S(1)} %copy-done.1), custom_call_target="tpu_custom_call" | custom-call | flops 2000000000 | bytes 4194304 | tf_op jit(solution)/shard_map/pallas_call | solution.py:239
  31.7 0.0 all-to-all-done.gathered
  31.8 0.0 copy-done
  31.8 0.0 copy-done.2
  31.8 2.1 %shard_map.95.far = f32[64,256]{1,0:T(8,128)S(1)} custom-call(s32[4,4]{1,0:T(4,128)} %tops_hbm.1, bf16[64,16,128]{2,1,0:T(8,128)(2,1)S(1)} %all-to-all-done.gathered, bf16[4,4,2,128,128]{4,3,2,1,0:T(8,128)(2,1)S(1)} %copy-done.2, bf16[16,2,128,128]{3,2,1,0:T(8,128)(2,1)S(1)} %copy-done, bf16[16,2,128,256]{3,2,1,0:T(8,128)(2,1)} %basis_hbm.3, ...), custom_call_target="tpu_custom_call" | custom-call | flops 2000000000 | bytes 4194304 | tf_op jit(solution)/shard_map/pallas_call | solution.py:239
  33.9 0.0 collective-permute-done.4.received
  33.9 0.6 %shard_map.96 = bf16[16,2,2,256]{3,2,1,0:T(2,128)(2,1)} custom-call(f32[64,256]{1,0:T(8,128)S(1)} %shard_map.95.far, f32[64,256]{1,0:T(8,128)S(1)} %get-tuple-element.25.mine, bf16[64,256]{1,0:T(8,128)(2,1)S(1)} %collective-permute-done.4.received), custom_call_target="tpu_custom_call" | custom-call | flops 10000000 | bytes 4194304 | tf_op jit(solution)/shard_map/pallas_call | solution.py:239
  (1 shorter events, 0.0 us)
Async XLA Ops:
  3.4 16.4 %collective-permute-start.2 = (bf16[576,128]{1,0:T(8,128)(2,1)S(1)}, bf16[576,128]{1,0:T(8,128)(2,1)S(1)}, u32[]{:S(2)}, u32[]{:S(2)}) collective-permute-start(bf16[576,128]{1,0:T(8,128)(2,1)S(1)} %get-tuple-element.18.message), channel_id=1, source_target_pairs={{4,8},{8,4},{12,16},{16,12},{20,24},{24,20},{28,32},{32,28},{36,40... | collective-permute-start | bytes 442376 | tf_op jit(solution)/shard_map/ppermute | solution.py:260
  4.1 15.7 %collective-permute-start.1 = (bf16[576,128]{1,0:T(8,128)(2,1)S(1)}, bf16[576,128]{1,0:T(8,128)(2,1)S(1)}, u32[]{:S(2)}, u32[]{:S(2)}) collective-permute-start(bf16[576,128]{1,0:T(8,128)(2,1)S(1)} %get-tuple-element.18.message), channel_id=1, source_target_pairs={{0,4},{4,0},{8,12},{12,8},{16,20},{20,16},{24,28},{28,24},{32,36},... | collective-permute-start | bytes 442376 | tf_op jit(solution)/shard_map/ppermute | solution.py:260
  8.7 23.1 %all-to-all-start = ((bf16[64,16,128]{2,1,0:T(8,128)(2,1)}), bf16[64,16,128]{2,1,0:T(8,128)(2,1)S(1)}, u32[]{:S(2)}, u32[]{:S(2)}) async-start(bf16[64,16,128]{2,1,0:T(8,128)(2,1)} %get-tuple-element.16), calls=%async_computation | async-start | bytes 524288 | tf_op jit(solution)/shard_map/all_to_all | solution.py:310
  22.3 8.3 %copy-start.1 = (bf16[16,4,2,128,128]{4,3,2,1,0:T(8,128)(2,1)S(1)}, bf16[16,4,2,128,128]{4,3,2,1,0:T(8,128)(2,1)}, u32[]{:S(2)}) copy-start(bf16[16,4,2,128,128]{4,3,2,1,0:T(8,128)(2,1)} %coupling.1) | copy-start | bytes 12582916
  22.3 3.9 %collective-permute-start.3 = (bf16[128,256]{1,0:T(8,128)(2,1)S(1)}, bf16[128,256]{1,0:T(8,128)(2,1)S(1)}, u32[]{:S(2)}, u32[]{:S(2)}) collective-permute-start(bf16[128,256]{1,0:T(8,128)(2,1)S(1)} %get-tuple-element.22), channel_id=1, source_target_pairs={{0,1},{1,0},{2,3},{3,2},{4,5},{5,4},{6,7},{7,6},{8,9},{9,8},{10,11... | collective-permute-start | bytes 196616 | tf_op jit(solution)/shard_map/ppermute | solution.py:265
  23.9 6.7 %collective-permute-start = (bf16[64,128]{1,0:T(8,128)(2,1)S(1)}, bf16[64,128]{1,0:T(8,128)(2,1)S(1)}, u32[]{:S(2)}, u32[]{:S(2)}) collective-permute-start(bf16[64,128]{1,0:T(8,128)(2,1)S(1)} %get-tuple-element.17), channel_id=1, source_target_pairs={{0,128},{4,132},{8,136},{12,140},{16,144},{20,148},{24,152},{28,15... | collective-permute-start | bytes 49160 | tf_op jit(solution)/shard_map/ppermute | solution.py:252
  26.2 5.5 %copy-start = (bf16[16,2,128,128]{3,2,1,0:T(8,128)(2,1)S(1)}, bf16[16,2,128,128]{3,2,1,0:T(8,128)(2,1)}, u32[]{:S(2)}) copy-start(bf16[16,2,128,128]{3,2,1,0:T(8,128)(2,1)} %transfer.1) | copy-start | bytes 3145732
  26.2 5.5 %copy-start.2 = (bf16[4,4,2,128,128]{4,3,2,1,0:T(8,128)(2,1)S(1)}, bf16[4,4,2,128,128]{4,3,2,1,0:T(8,128)(2,1)}, u32[]{:S(2)}) copy-start(bf16[4,4,2,128,128]{4,3,2,1,0:T(8,128)(2,1)} %top_coupling.1) | copy-start | bytes 3145732
  26.2 7.7 %collective-permute-start.4 = (bf16[64,256]{1,0:T(8,128)(2,1)S(1)}, bf16[64,256]{1,0:T(8,128)(2,1)S(1)}, u32[]{:S(2)}, u32[]{:S(2)}) collective-permute-start(bf16[64,256]{1,0:T(8,128)(2,1)S(1)} %get-tuple-element.26), channel_id=1, source_target_pairs={{0,2},{1,3},{2,0},{3,1},{4,6},{5,7},{6,4},{7,5},{8,10},{9,11},{10,... | collective-permute-start | bytes 98312 | tf_op jit(solution)/shard_map/ppermute | solution.py:265

commit v6 on v5

--- a/solution.py
+++ b/solution.py
@@ -103,7 +103,6 @@
     size = message.shape[0] - span
     each = size // leaves
     count = each // 2
-    lists = Stream([(near_hbm, near_list), (places_hbm, places)], listed, 2)
     step = 4
     begin = early.shape[0]
     stream = Stream(
@@ -114,6 +113,7 @@
         arrived,
         4,
     )
+    lists = Stream([(near_hbm, near_list), (places_hbm, places)], listed, 2)
     me = lax.axis_index("leaf")
     order = ((even_side, 2 - 2 * (me % 2)), (message, 1), (odd_side, 2 * (me % 2)))
     tables = Stream(

time: 34.8 us -> 34.8 us (level)
  no operation moved by 1% of the time
where the time goes in v6:
time: 34.8 us; the launch traced here: 34.6 us
  starting transfers between devices  24.6 us (71%)
  Pallas kernels  9.82 us (28%)
    all_to_all x1, starting transfers between devices, local(): gathered = lax.all_to_all(parents, 'leaf', 0, 0, tiled=True)  11.1 us
    pallas_call x6, Pallas kernels, call(): pl.pallas_call(kernel, out_shape=[jax.ShapeDtypeStruct(*shape) for shape...  9.82 us
    ppermute x2, starting transfers between devices, flipped(): return lax.ppermute(value, axis, [(i, i ^ bit) for i in range(count)])  5.9 us
    ppermute x2, starting transfers between devices, paired(): return lax.ppermute(value, axis, pairs)  5.25 us
    ppermute x1, starting transfers between devices, shifted(): lax.ppermute(value, axis, [(i, (i - step) % count) for i in range(count)])  2.31 us
  transfers between devices with their start and end apart: 6, of which 0 were waited for; matrix products, arithmetic and copies ran while one was open for 0% of the time, Pallas kernels for 17%

profile of v6, /device:TPU:1, one launch (start us, length us, event | category | flops | bytes accessed | tf_op | source)
XLA Modules:
  0.0 34.6 jit_solution(14107791223636098927)
XLA Ops:
  0.0 3.4 %shard_map.91 = (bf16[64,16,128]{2,1,0:T(8,128)(2,1)}, bf16[64,128]{1,0:T(8,128)(2,1)S(1)}, bf16[576,128]{1,0:T(8,128)(2,1)S(1)}, bf16[8,1,2,256,256]{4,3,2,1,0:T(8,128)(2,1)S(1)}) custom-call(bf16[16,8,2,256]{3,2,1,0:T(2,128)(2,1)} %charges_hbm.1, bf16[16,2,128,256]{3,2,1,0:T(8,128)(2,1)} %basis_hbm.3, bf16[16,2,128,128]{3,2,1,0:T(8,128)(2,1)} %transfer.1, ...), custom_call_target="tpu_custom_call" | custom-call | flops 200000000 | bytes 4194304 | tf_op jit(solution)/shard_map/pallas_call | solution.py:239
  3.4 0.7 %collective-permute-start.2 = (bf16[576,128]{1,0:T(8,128)(2,1)S(1)}, bf16[576,128]{1,0:T(8,128)(2,1)S(1)}, u32[]{:S(2)}, u32[]{:S(2)}) collective-permute-start(bf16[576,128]{1,0:T(8,128)(2,1)S(1)} %get-tuple-element.18.message), channel_id=1, source_target_pairs={{4,8},{8,4},{12,16},{16,12},{20,24},{24,20},{28,32},{32,28},{36,40... | collective-permute-start | bytes 442376 | tf_op jit(solution)/shard_map/ppermute | solution.py:260
  4.1 4.6 %collective-permute-start.1 = (bf16[576,128]{1,0:T(8,128)(2,1)S(1)}, bf16[576,128]{1,0:T(8,128)(2,1)S(1)}, u32[]{:S(2)}, u32[]{:S(2)}) collective-permute-start(bf16[576,128]{1,0:T(8,128)(2,1)S(1)} %get-tuple-element.18.message), channel_id=1, source_target_pairs={{0,4},{4,0},{8,12},{12,8},{16,20},{20,16},{24,28},{28,24},{32,36},... | collective-permute-start | bytes 442376 | tf_op jit(solution)/shard_map/ppermute | solution.py:260
  8.7 11.1 %all-to-all-start = ((bf16[64,16,128]{2,1,0:T(8,128)(2,1)}), bf16[64,16,128]{2,1,0:T(8,128)(2,1)S(1)}, u32[]{:S(2)}, u32[]{:S(2)}) async-start(bf16[64,16,128]{2,1,0:T(8,128)(2,1)} %get-tuple-element.16), calls=%async_computation | async-start | bytes 524288 | tf_op jit(solution)/shard_map/all_to_all | solution.py:310
  19.8 0.0 collective-permute-done.2.odd_side
  19.8 0.0 collective-permute-done.1.even_side
  19.9 2.4 %shard_map.92 = (f32[128,256]{1,0:T(8,128)S(1)}, bf16[128,256]{1,0:T(8,128)(2,1)S(1)}, f32[64,384]{1,0:T(8,128)S(1)}) custom-call(s32[1,16]{1,0:T(1,128)} %bitcast.3, s32[4,16]{1,0:T(4,128)} %bitcast.2, bf16[576,128]{1,0:T(8,128)(2,1)S(1)} %get-tuple-element.18.message, bf16[576,128]{1,0:T(8,128)(2,1)S(1)} %collective-permute-done.1.even_side, ...), custom_call_target="tpu_custom_call" | custom-call | flops 2000000000 | bytes 4194304 | tf_op jit(solution)/shard_map/pallas_call | solution.py:239
  22.3 0.0 copy-start.1
  22.3 1.6 %collective-permute-start.3 = (bf16[128,256]{1,0:T(8,128)(2,1)S(1)}, bf16[128,256]{1,0:T(8,128)(2,1)S(1)}, u32[]{:S(2)}, u32[]{:S(2)}) collective-permute-start(bf16[128,256]{1,0:T(8,128)(2,1)S(1)} %get-tuple-element.22), channel_id=1, source_target_pairs={{0,1},{1,0},{2,3},{3,2},{4,5},{5,4},{6,7},{7,6},{8,9},{9,8},{10,11... | collective-permute-start | bytes 196616 | tf_op jit(solution)/shard_map/ppermute | solution.py:265
  23.9 2.3 %collective-permute-start = (bf16[64,128]{1,0:T(8,128)(2,1)S(1)}, bf16[64,128]{1,0:T(8,128)(2,1)S(1)}, u32[]{:S(2)}, u32[]{:S(2)}) collective-permute-start(bf16[64,128]{1,0:T(8,128)(2,1)S(1)} %get-tuple-element.17), channel_id=1, source_target_pairs={{0,128},{4,132},{8,136},{12,140},{16,144},{20,148},{24,152},{28,15... | collective-permute-start | bytes 49160 | tf_op jit(solution)/shard_map/ppermute | solution.py:252
  26.2 0.0 collective-permute-done.3.received
  26.2 0.0 copy-start
  26.2 0.0 copy-start.2
  26.2 4.3 %collective-permute-start.4 = (bf16[64,256]{1,0:T(8,128)(2,1)S(1)}, bf16[64,256]{1,0:T(8,128)(2,1)S(1)}, u32[]{:S(2)}, u32[]{:S(2)}) collective-permute-start(bf16[64,256]{1,0:T(8,128)(2,1)S(1)} %get-tuple-element.26), channel_id=1, source_target_pairs={{0,2},{1,3},{2,0},{3,1},{4,6},{5,7},{6,4},{7,5},{8,10},{9,11},{10,... | collective-permute-start | bytes 98312 | tf_op jit(solution)/shard_map/ppermute | solution.py:265
  30.5 0.0 collective-permute-done.distant
  30.5 0.0 copy-done.1
  30.5 1.2 %shard_map.94.field = f32[64,128]{1,0:T(8,128)S(1)} custom-call(bf16[64,128]{1,0:T(8,128)(2,1)S(1)} %collective-permute-done.distant, f32[64,384]{1,0:T(8,128)S(1)} %get-tuple-element.24.sources, bf16[16,4,2,128,128]{4,3,2,1,0:T(8,128)(2,1)S(1)} %copy-done.1), custom_call_target="tpu_custom_call" | custom-call | flops 2000000000 | bytes 4194304 | tf_op jit(solution)/shard_map/pallas_call | solution.py:239
  31.7 0.0 all-to-all-done.gathered
  31.8 0.0 copy-done
  31.8 0.0 copy-done.2
  31.8 2.1 %shard_map.95.far = f32[64,256]{1,0:T(8,128)S(1)} custom-call(s32[4,4]{1,0:T(4,128)} %tops_hbm.1, bf16[64,16,128]{2,1,0:T(8,128)(2,1)S(1)} %all-to-all-done.gathered, bf16[4,4,2,128,128]{4,3,2,1,0:T(8,128)(2,1)S(1)} %copy-done.2, bf16[16,2,128,128]{3,2,1,0:T(8,128)(2,1)S(1)} %copy-done, bf16[16,2,128,256]{3,2,1,0:T(8,128)(2,1)} %basis_hbm.3, ...), custom_call_target="tpu_custom_call" | custom-call | flops 2000000000 | bytes 4194304 | tf_op jit(solution)/shard_map/pallas_call | solution.py:239
  33.9 0.0 collective-permute-done.4.received
  33.9 0.6 %shard_map.96 = bf16[16,2,2,256]{3,2,1,0:T(2,128)(2,1)} custom-call(f32[64,256]{1,0:T(8,128)S(1)} %shard_map.95.far, f32[64,256]{1,0:T(8,128)S(1)} %get-tuple-element.25.mine, bf16[64,256]{1,0:T(8,128)(2,1)S(1)} %collective-permute-done.4.received), custom_call_target="tpu_custom_call" | custom-call | flops 10000000 | bytes 4194304 | tf_op jit(solution)/shard_map/pallas_call | solution.py:239
  (1 shorter events, 0.0 us)
Async XLA Ops:
  3.4 16.4 %collective-permute-start.2 = (bf16[576,128]{1,0:T(8,128)(2,1)S(1)}, bf16[576,128]{1,0:T(8,128)(2,1)S(1)}, u32[]{:S(2)}, u32[]{:S(2)}) collective-permute-start(bf16[576,128]{1,0:T(8,128)(2,1)S(1)} %get-tuple-element.18.message), channel_id=1, source_target_pairs={{4,8},{8,4},{12,16},{16,12},{20,24},{24,20},{28,32},{32,28},{36,40... | collective-permute-start | bytes 442376 | tf_op jit(solution)/shard_map/ppermute | solution.py:260
  4.1 15.7 %collective-permute-start.1 = (bf16[576,128]{1,0:T(8,128)(2,1)S(1)}, bf16[576,128]{1,0:T(8,128)(2,1)S(1)}, u32[]{:S(2)}, u32[]{:S(2)}) collective-permute-start(bf16[576,128]{1,0:T(8,128)(2,1)S(1)} %get-tuple-element.18.message), channel_id=1, source_target_pairs={{0,4},{4,0},{8,12},{12,8},{16,20},{20,16},{24,28},{28,24},{32,36},... | collective-permute-start | bytes 442376 | tf_op jit(solution)/shard_map/ppermute | solution.py:260
  8.7 23.1 %all-to-all-start = ((bf16[64,16,128]{2,1,0:T(8,128)(2,1)}), bf16[64,16,128]{2,1,0:T(8,128)(2,1)S(1)}, u32[]{:S(2)}, u32[]{:S(2)}) async-start(bf16[64,16,128]{2,1,0:T(8,128)(2,1)} %get-tuple-element.16), calls=%async_computation | async-start | bytes 524288 | tf_op jit(solution)/shard_map/all_to_all | solution.py:310
  22.3 8.3 %copy-start.1 = (bf16[16,4,2,128,128]{4,3,2,1,0:T(8,128)(2,1)S(1)}, bf16[16,4,2,128,128]{4,3,2,1,0:T(8,128)(2,1)}, u32[]{:S(2)}) copy-start(bf16[16,4,2,128,128]{4,3,2,1,0:T(8,128)(2,1)} %coupling.1) | copy-start | bytes 12582916
  22.3 3.9 %collective-permute-start.3 = (bf16[128,256]{1,0:T(8,128)(2,1)S(1)}, bf16[128,256]{1,0:T(8,128)(2,1)S(1)}, u32[]{:S(2)}, u32[]{:S(2)}) collective-permute-start(bf16[128,256]{1,0:T(8,128)(2,1)S(1)} %get-tuple-element.22), channel_id=1, source_target_pairs={{0,1},{1,0},{2,3},{3,2},{4,5},{5,4},{6,7},{7,6},{8,9},{9,8},{10,11... | collective-permute-start | bytes 196616 | tf_op jit(solution)/shard_map/ppermute | solution.py:265
  23.9 6.7 %collective-permute-start = (bf16[64,128]{1,0:T(8,128)(2,1)S(1)}, bf16[64,128]{1,0:T(8,128)(2,1)S(1)}, u32[]{:S(2)}, u32[]{:S(2)}) collective-permute-start(bf16[64,128]{1,0:T(8,128)(2,1)S(1)} %get-tuple-element.17), channel_id=1, source_target_pairs={{0,128},{4,132},{8,136},{12,140},{16,144},{20,148},{24,152},{28,15... | collective-permute-start | bytes 49160 | tf_op jit(solution)/shard_map/ppermute | solution.py:252
  26.2 5.5 %copy-start = (bf16[16,2,128,128]{3,2,1,0:T(8,128)(2,1)S(1)}, bf16[16,2,128,128]{3,2,1,0:T(8,128)(2,1)}, u32[]{:S(2)}) copy-start(bf16[16,2,128,128]{3,2,1,0:T(8,128)(2,1)} %transfer.1) | copy-start | bytes 3145732
  26.2 5.5 %copy-start.2 = (bf16[4,4,2,128,128]{4,3,2,1,0:T(8,128)(2,1)S(1)}, bf16[4,4,2,128,128]{4,3,2,1,0:T(8,128)(2,1)}, u32[]{:S(2)}) copy-start(bf16[4,4,2,128,128]{4,3,2,1,0:T(8,128)(2,1)} %top_coupling.1) | copy-start | bytes 3145732
  26.2 7.7 %collective-permute-start.4 = (bf16[64,256]{1,0:T(8,128)(2,1)S(1)}, bf16[64,256]{1,0:T(8,128)(2,1)S(1)}, u32[]{:S(2)}, u32[]{:S(2)}) collective-permute-start(bf16[64,256]{1,0:T(8,128)(2,1)S(1)} %get-tuple-element.26), channel_id=1, source_target_pairs={{0,2},{1,3},{2,0},{3,1},{4,6},{5,7},{6,4},{7,5},{8,10},{9,11},{10,... | collective-permute-start | bytes 98312 | tf_op jit(solution)/shard_map/ppermute | solution.py:265
